TPU v7x, 32 devices: a whole 2x2x4 slice. The times are simulated.
32 devices in a mesh: stn: 16 (over z, x, core), elem: 2 (over y).
Axes of the slice: x: 2, y: 2, z: 4, core: 2. Of those that a mesh axis runs over, the one named last changes fastest.
Arguments:
- voltages: bfloat16 [2, 16, 64, 16, 128], P(None, 'stn', 'elem'), may hold values from -6 to 6
- weights: bfloat16 [2, 8, 64, 16], P(None, None, 'elem'), may hold values from -0.5 to 0.5
Outputs:
- spectra: float32 [2, 16, 128, 128], P(None, 'elem', 'stn')
All inputs are finite; a program needn't handle non-finite values.
Results may differ from a plain program's by a relative error of at most 0.0075.
Values may be sent and summed in bfloat16 or wider, within the bound.
No kernel may reach another device: no remote copies, remote signals or barrier semaphores. Data moves between devices by JAX's collectives and lax.ppermute only.
A program may use at most 64 MiB of HBM per device.

v0:
```python
import jax
import jax.numpy as jnp
from jax import lax
from jax.sharding import PartitionSpec as P


def form_beams(voltages, weights):
    real_part = jnp.einsum(
        "kec,sect->sckt", weights[0], voltages[0], preferred_element_type=jnp.float32
    ) + jnp.einsum("kec,sect->sckt", weights[1], voltages[1], preferred_element_type=jnp.float32)
    imag_part = jnp.einsum(
        "kec,sect->sckt", weights[0], voltages[1], preferred_element_type=jnp.float32
    ) - jnp.einsum("kec,sect->sckt", weights[1], voltages[0], preferred_element_type=jnp.float32)
    return jnp.stack([real_part, imag_part])


def row_folder(mine, piece):
    spec_real = jnp.einsum(
        "cit,cjt->cij", mine[0], piece[0], preferred_element_type=jnp.float32
    ) + jnp.einsum("cit,cjt->cij", mine[1], piece[1], preferred_element_type=jnp.float32)
    spec_imag = jnp.einsum(
        "cit,cjt->cij", mine[1], piece[0], preferred_element_type=jnp.float32
    ) - jnp.einsum("cit,cjt->cij", mine[0], piece[1], preferred_element_type=jnp.float32)
    return jnp.stack([spec_real, spec_imag])


def body(voltages, weights):
    partial_beams = form_beams(voltages, weights)
    samples = voltages.shape[4]
    summed = lax.psum_scatter(partial_beams, "elem", scatter_dimension=2, tiled=True)
    mine = summed.astype(jnp.bfloat16)[:, 0]
    spectra = row_folder(mine, lax.all_gather(mine, "stn", axis=2, tiled=True))
    return spectra / jnp.float32(samples)


def solution(mesh):
    placed = (P(None, "stn", "elem", None, None), P(None, None, "elem", None))
    return jax.shard_map(
        body, mesh=mesh, in_specs=placed, out_specs=P(None, "elem", "stn", None), check_vma=False
    )
```

profile of v0, /device:TPU:0, one launch (start us, length us, event | category | flops | bytes accessed | tf_op | source)
XLA Modules:
  0.0 55.0 jit_solution(4943786876155844651)
XLA Ops:
  6.5 0.0 reduce-scatter.5.cloned.1.call-start
  6.5 0.8 %fusion.9 = (bf16[1,8,32,16]{2,3,1,0:T(8,128)(2,1)S(1)}, bf16[1,8,32,16]{2,3,1,0:T(8,128)(2,1)S(1)}) fusion(bf16[2,8,32,16]{2,3,1,0:T(8,128)(2,1)} %param.3), kind=kLoop, calls=%fused_computation.26 | loop fusion | bytes 32768 | tf_op jit(solution)/shard_map/slice | solution.py:10
  7.3 1.0 %fusion.8 = (bf16[1,1,32,16,128]{4,3,2,1,0:T(8,128)(2,1)S(1)}, bf16[1,1,32,16,128]{4,3,2,1,0:T(8,128)(2,1)S(1)}) fusion(bf16[2,1,32,16,128]{4,3,2,1,0:T(8,128)(2,1)} %param.2), kind=kLoop, calls=%fused_computation.25 | loop fusion | bytes 524288 | tf_op jit(solution)/shard_map/slice | solution.py:9
  8.3 0.2 fusion.6
  8.5 0.2 fusion.7
  8.6 0.2 fusion.1
  8.8 0.2 fusion
  9.0 0.7 %copy.47 = f32[2,8,16,128]{3,1,2,0:T(8,128)} copy(f32[2,8,16,128]{3,2,1,0:T(8,128)S(1)} %bitcast.65) | data formatting | bytes 262144
  9.7 0.0 reduce-scatter.5.cloned.1.call-update
  9.7 13.1 %reduce-scatter.5.cloned.1.call-done = f32[8,2048]{1,0:T(8,128)} async-done(((f32[16,2048]{1,0:T(8,128)}), f32[8,2048]{1,0:T(8,128)}) %reduce-scatter.5.cloned.1.call-update) | async-done | bytes 65552
  22.8 0.9 %copy.48 = bf16[1,8,16,128]{3,2,1,0:T(8,128)(2,1)S(1)} copy(f32[1,8,16,128]{3,1,2,0:T(8,128)} %bitcast.71) | data formatting | bytes 98304
  23.7 22.8 %all-gather = bf16[2,1,8,128,128]{4,3,2,1,0:T(8,128)(2,1)S(1)} all-gather(bf16[2,1,8,8,128]{4,3,2,1,0:T(8,128)(2,1)S(1)} %copy.34), channel_id=2, replica_groups=mesh['stn'=16,'elem'=2] {'stn'}, dimensions={3}, use_global_device_ids=true | all-gather | bytes 557056 | tf_op jit(solution)/shard_map/all_gather | solution.py:32
  46.5 0.2 fusion.4
  46.7 0.2 fusion.5
  47.0 0.2 fusion.2
  47.2 0.2 fusion.3
  47.5 0.7 %maximum_multiply_fusion = f32[2,8,8,128]{3,2,1,0:T(8,128)} fusion(f32[1,8,8,128]{3,2,1,0:T(8,128)S(1)} %fusion.2, f32[1,8,8,128]{3,2,1,0:T(8,128)S(1)} %fusion.3), kind=kLoop, calls=%fused_computation.19 | loop fusion | flops 32768 | bytes 131072 | tf_op jit(solution)/shard_map/div | solution.py:33
  (3 shorter events, 0.0 us)
Async XLA Ops:
  6.5 16.3 %reduce-scatter.5.cloned.1.call-start = ((), (), s32[]{:S(2)}) async-start(), calls=%async_computation.1 | async-start | bytes 196608
Sparse Core Ops, SparseCore 0:
  9.8 12.9 reduce-scatter.4
where the time goes:
time: 55.2 us; the launch traced here: 55 us
  blocking collectives  22.8 us (41%)
  between operations  13.4 us (24%)
  waiting for transfers between devices  13.1 us (24%)
  local copies, waits for them, and re-layouts  3.32 us (6%)
  matrix products  1.6 us (3%)
  other arithmetic  0.67 us (1%)
    all_gather x1, blocking collectives, body(): spectra = row_folder(mine, lax.all_gather(mine, 'stn', axis=2, tiled=True))  22.8 us
    unnamed x2, waiting for transfers between devices  13.1 us
    unnamed x4, local copies, waits for them, and re-layouts  1.56 us
  transfers between devices with their start and end apart: 1, of which 1 were waited for; matrix products, arithmetic and copies ran while one was open for 0% of the time, Pallas kernels for 0%

commit v1 on v0

v1 whole, which is shorter than its diff:
```python
import functools

import jax
import jax.numpy as jnp
from jax import lax
from jax.experimental import pallas as pl
from jax.experimental.pallas import tpu as pltpu
from jax.sharding import PartitionSpec as P


def beam_kernel(parts, v_ref, w_ref, mine_ref, send_ref, w32, both):
    planes, elems, chans, samples = v_ref.shape
    rows = w_ref.shape[0] // chans
    deep = elems * chans
    w32[...] = w_ref[...].astype(jnp.float32)
    by_channel = jnp.concatenate([w32[pl.ds(c, rows, stride=chans), :] for c in range(chans)])
    lane = lax.broadcasted_iota(jnp.int32, (elems, deep), 1)
    low = lax.broadcasted_iota(jnp.int32, (elems, deep), 0) * chans
    spread = jnp.where((lane >= low) & (lane < low + chans), 1.0, 0.0).astype(jnp.bfloat16)
    wide = jnp.dot(by_channel.astype(jnp.bfloat16), spread, preferred_element_type=jnp.float32)
    wide = wide.reshape(chans, rows, deep)
    lane = lax.rem(lax.broadcasted_iota(jnp.int32, wide.shape, 2), chans)
    wide = jnp.where(lane == lax.broadcasted_iota(jnp.int32, wide.shape, 0), wide, 0.0)
    wide = wide.reshape(chans * rows, deep).astype(jnp.bfloat16)
    volts = v_ref[...].reshape(planes, deep, samples)
    half = rows // 2
    by_real = jnp.dot(wide, volts[0], preferred_element_type=jnp.float32).reshape(chans, 2, half, samples)
    by_imag = jnp.dot(wide, volts[1], preferred_element_type=jnp.float32).reshape(chans, 2, half, samples)
    both[:, 0] = by_real[:, 0] + by_imag[:, 1]
    both[:, 1] = by_imag[:, 0] - by_real[:, 1]
    owned = chans // parts
    me = lax.axis_index("elem")
    mine_ref[...] = both[pl.ds(me * owned, owned)].reshape(mine_ref.shape)
    for step in range(1, parts):
        other = lax.rem(me + step, parts) * owned
        send_ref[step - 1] = both[pl.ds(other, owned)].reshape(mine_ref.shape).astype(jnp.bfloat16)


def partial_beams(voltages, weights, parts):
    planes, _, elems, chans, samples = voltages.shape
    rows = planes * weights.shape[1]
    owned = chans // parts
    return pl.pallas_call(
        functools.partial(beam_kernel, parts),
        out_shape=(
            jax.ShapeDtypeStruct((owned, rows, samples), jnp.float32),
            jax.ShapeDtypeStruct((parts - 1, owned, rows, samples), jnp.bfloat16),
        ),
        scratch_shapes=[
            pltpu.VMEM((rows * chans, elems), jnp.float32),
            pltpu.VMEM((chans, planes, rows // planes, samples), jnp.float32),
        ],
    )(voltages[:, 0], weights.transpose(0, 1, 3, 2).reshape(rows * chans, elems))


def spectra_kernel(order, *refs):
    blocks, out_ref = refs[:-1], refs[-1]
    chans, rows, samples = blocks[0].shape[1:]
    half = rows // 2
    where = [(ref, i) for ref in blocks for i in range(ref.shape[0])]
    me = lax.axis_index("stn")
    found = []
    for c in range(chans):
        tiles = [where[k][0][where[k][1], c].astype(jnp.float32) for k in order]
        real = jnp.concatenate([t[:half] for t in tiles]).astype(jnp.bfloat16)
        imag = jnp.concatenate([t[half:] for t in tiles]).astype(jnp.bfloat16)
        own = tiles[0]
        left = jnp.concatenate([own, jnp.concatenate([own[half:], -own[:half]])], axis=1)
        right = jnp.concatenate([real, imag], axis=1)
        found.append(
            lax.dot_general(
                left.astype(jnp.bfloat16), right, (((1,), (1,)), ((), ())),
                preferred_element_type=jnp.float32,
            )
        )
    spec = jnp.concatenate(found)
    beams = spec.shape[1]
    lane = lax.broadcasted_iota(jnp.int32, spec.shape, 1)
    bit, width = 1, half
    while width < beams:
        if width < 128:
            moved = jnp.where(
                lane & width == 0, pltpu.roll(spec, beams - width, 1), pltpu.roll(spec, width, 1)
            )
        else:
            cuts = [spec[:, at : at + width] for at in range(0, beams, width)]
            moved = jnp.concatenate([cuts[i ^ 1] for i in range(len(cuts))], axis=1)
        spec = jnp.where(me & bit != 0, moved, spec)
        bit, width = bit * 2, width * 2
    spec = spec.reshape(chans, 2, half, beams) / jnp.float32(samples)
    out_ref[0] = spec[:, 0]
    out_ref[1] = spec[:, 1]


def cross_spectra(blocks, offsets):
    chans, rows, samples = blocks[0].shape[1:]
    stations = len(offsets)
    order = [offsets.index(d) for d in range(stations)]
    return pl.pallas_call(
        functools.partial(spectra_kernel, order),
        out_shape=jax.ShapeDtypeStruct((2, chans, rows // 2, stations * (rows // 2)), jnp.float32),
    )(*blocks)


def body(steps, stations, parts, voltages, weights):
    mine, sent = partial_beams(voltages, weights, parts)
    for step in range(1, parts):
        pairs = [(i, (i + step) % parts) for i in range(parts)]
        mine = mine + lax.ppermute(sent[step - 1], "elem", pairs).astype(jnp.float32)
    held = mine.astype(jnp.bfloat16)[None]
    offsets = [0]
    for step in steps[:-1]:
        got = lax.ppermute(held, "stn", [(i, i ^ step) for i in range(stations)])
        held = jnp.concatenate([held, got])
        offsets += [o ^ step for o in offsets]
    step = steps[-1]
    got = lax.ppermute(held, "stn", [(i, i ^ step) for i in range(stations)])
    offsets += [o ^ step for o in offsets]
    return cross_spectra([held, got], offsets)


def solution(mesh):
    stations, parts = mesh.shape["stn"], mesh.shape["elem"]
    steps = []
    bit = stations // 2
    while bit > 1:
        steps.append(bit + 1)
        bit //= 2
    steps.append(1)
    placed = (P(None, "stn", "elem", None, None), P(None, None, "elem", None))
    return jax.shard_map(
        functools.partial(body, steps, stations, parts),
        mesh=mesh, in_specs=placed, out_specs=P(None, "elem", "stn", None), check_vma=False,
    )
```

time: 55.2 us -> 26.7 us (0.48)
  blocking collectives: 22.8 us -> 0 us
  between operations: 13.4 us -> 0.03 us
  starting transfers between devices: 0.01 us -> 8.64 us
  Pallas kernels: 0 us -> 4.24 us
  local copies, waits for them, and re-layouts: 3.32 us -> 0.7 us
  matrix products: 1.6 us -> 0 us
  waiting for transfers between devices: 13.1 us -> 12 us
    all_gather x1 -> x0, blocking collectives: 22.8 us -> none  [body(): spectra = row_folder(mine, lax.all_gather(mine, 'stn', axis=2, tiled=True))]
    unnamed x2 -> x0, waiting for transfers between devices: 13.1 us -> none
    ppermute x0 -> x5, waiting for transfers between devices: none -> 12 us  [the longest x4 9.89 us: body(): got = lax.ppermute(held, 'stn', [(i, i ^ step) for i in range(stations)])]
    ppermute x0 -> x5, starting transfers between devices: none -> 8.64 us  [the longest x4 5.67 us: body(): got = lax.ppermute(held, 'stn', [(i, i ^ step) for i in range(stations)])]
    pallas_call x0 -> x2, Pallas kernels: none -> 4.24 us  [the longest x1 2.2 us: cross_spectra(): pl.pallas_call(functools.partial(spectra_kernel, order), out_shape=jax.Sh...]
    slice x2 -> x0, local copies, waits for them, and re-layouts: 1.76 us -> none  [the longest x1 0.99 us: form_beams(): voltages[0]]
    dot_general x8 -> x0, matrix products: 1.6 us -> none  [the longest x1 0.25 us: row_folder(): jnp.einsum('cit,cjt->cij', mine[0], piece[1], preferred_element_type=jnp....]
    unnamed x4, local copies, waits for them, and re-layouts: 1.56 us -> 0.7 us
  transfers between devices with their start and end apart: 1 -> 5, of which waited for: 1 -> 5; matrix products, arithmetic and copies ran while one was open for 0% -> 0% of each run, Pallas kernels for 0% -> 0%
where the time goes in v1:
time: 26.7 us; the launch traced here: 26.5 us
  waiting for transfers between devices  12 us (45%)
  starting transfers between devices  8.64 us (32%)
  Pallas kernels  4.24 us (16%)
  other arithmetic  0.9 us (3%)
  local copies, waits for them, and re-layouts  0.7 us (3%)
    ppermute x4, waiting for transfers between devices, body(): got = lax.ppermute(held, 'stn', [(i, i ^ step) for i in range(stations)])  9.89 us
    ppermute x4, starting transfers between devices, body(): got = lax.ppermute(held, 'stn', [(i, i ^ step) for i in range(stations)])  5.67 us
    ppermute x1, starting transfers between devices, body(): lax.ppermute(sent[step - 1], 'elem', pairs).astype(jnp.float32)  2.97 us
    pallas_call x1, Pallas kernels, cross_spectra(): pl.pallas_call(functools.partial(spectra_kernel, order), out_shape=jax.Sh...  2.2 us
    ppermute x1, waiting for transfers between devices, body(): lax.ppermute(sent[step - 1], 'elem', pairs).astype(jnp.float32)  2.1 us
    pallas_call x1, Pallas kernels, partial_beams(): pl.pallas_call(functools.partial(beam_kernel, parts), out_shape=(jax.Shap...  2.04 us
    broadcast_in_dim x1, other arithmetic, body(): held = mine.astype(jnp.bfloat16)[None]  0.85 us
    unnamed x4, local copies, waits for them, and re-layouts  0.7 us
  transfers between devices with their start and end apart: 5, of which 5 were waited for; matrix products, arithmetic and copies ran while one was open for 0% of the time, Pallas kernels for 0%

profile of v1, /device:TPU:0, one launch (start us, length us, event | category | flops | bytes accessed | tf_op | source)
XLA Modules:
  0.0 26.5 jit_solution(9873205750667637945)
XLA Ops:
  0.0 2.0 %shard_map.28 = (f32[8,16,128]{2,1,0:T(8,128)}, bf16[1,8,16,128]{3,2,1,0:T(8,128)(2,1)}) custom-call(bf16[2,32,16,128]{3,2,1,0:T(8,128)(2,1)} %bitcast.7, bf16[256,32]{1,0:T(8,128)(2,1)} %bitcast.8), custom_call_target="tpu_custom_call" | custom-call | tf_op jit(solution)/shard_map/pallas_call | solution.py:43
  2.0 3.0 %collective-permute-start = (bf16[8,16,128]{2,1,0:T(8,128)(2,1)}, bf16[8,16,128]{2,1,0:T(8,128)(2,1)S(1)}, u32[]{:S(2)}, u32[]{:S(2)}) collective-permute-start(bf16[8,16,128]{2,1,0:T(8,128)(2,1)} %bitcast.9), channel_id=1, source_target_pairs={{0,1},{1,0},{2,3},{3,2},{4,5},{5,4},{6,7},{7,6},{8,9},{9,8},{10,11... | collective-permute-start | bytes 98312 | tf_op jit(solution)/shard_map/ppermute | solution.py:109
  5.0 2.1 %collective-permute-done = bf16[8,16,128]{2,1,0:T(8,128)(2,1)S(1)} collective-permute-done((bf16[8,16,128]{2,1,0:T(8,128)(2,1)}, bf16[8,16,128]{2,1,0:T(8,128)(2,1)S(1)}, u32[]{:S(2)}, u32[]{:S(2)}) %collective-permute-start) | collective-permute-done | bytes 32800 | tf_op jit(solution)/shard_map/ppermute | solution.py:109
  7.1 0.8 %fusion = bf16[1,8,16,128]{3,2,1,0:T(8,128)(2,1)S(1)} fusion(f32[8,16,128]{2,1,0:T(8,128)} %get-tuple-element.7, bf16[8,16,128]{2,1,0:T(8,128)(2,1)S(1)} %collective-permute-done), kind=kLoop, calls=%fused_computation.4 | loop fusion | flops 49152 | bytes 131072 | tf_op jit(solution)/shard_map/broadcast_in_dim | solution.py:110
  8.0 1.5 %collective-permute-start.1 = (bf16[1,8,16,128]{3,2,1,0:T(8,128)(2,1)S(1)}, bf16[1,8,16,128]{3,2,1,0:T(8,128)(2,1)S(1)}, u32[]{:S(2)}, u32[]{:S(2)}) collective-permute-start(bf16[1,8,16,128]{3,2,1,0:T(8,128)(2,1)S(1)} %fusion), channel_id=1, source_target_pairs={{0,18},{2,16},{4,22},{6,20},{8,26},{10,24},{12,30},{14,28},{16,2},... | collective-permute-start | bytes 98312 | tf_op jit(solution)/shard_map/ppermute | solution.py:113
  9.4 2.8 %collective-permute-done.1 = bf16[1,8,16,128]{3,2,1,0:T(8,128)(2,1)S(1)} collective-permute-done((bf16[1,8,16,128]{3,2,1,0:T(8,128)(2,1)S(1)}, bf16[1,8,16,128]{3,2,1,0:T(8,128)(2,1)S(1)}, u32[]{:S(2)}, u32[]{:S(2)}) %collective-permute-start.1) | collective-permute-done | bytes 32800 | tf_op jit(solution)/shard_map/ppermute | solution.py:113
  12.3 2.0 %collective-permute-start.2 = (bf16[2,8,16,128]{3,2,1,0:T(8,128)(2,1)S(1)}, bf16[2,8,16,128]{3,2,1,0:T(8,128)(2,1)S(1)}, u32[]{:S(2)}, u32[]{:S(2)}) collective-permute-start(bf16[2,8,16,128]{3,2,1,0:T(8,128)(2,1)S(1)} %pad_maximum_fusion.2), channel_id=1, source_target_pairs={{0,10},{2,8},{4,14},{6,12},{8,2},{10,0},{12,6},{14,4},{16,26},{18,... | collective-permute-start | bytes 196616 | tf_op jit(solution)/shard_map/ppermute | solution.py:113
  14.3 2.2 %collective-permute-done.2 = bf16[2,8,16,128]{3,2,1,0:T(8,128)(2,1)S(1)} collective-permute-done((bf16[2,8,16,128]{3,2,1,0:T(8,128)(2,1)S(1)}, bf16[2,8,16,128]{3,2,1,0:T(8,128)(2,1)S(1)}, u32[]{:S(2)}, u32[]{:S(2)}) %collective-permute-start.2) | collective-permute-done | bytes 65568 | tf_op jit(solution)/shard_map/ppermute | solution.py:113
  16.5 1.9 %collective-permute-start.3 = (bf16[4,8,16,128]{3,2,1,0:T(8,128)(2,1)S(1)}, bf16[4,8,16,128]{3,2,1,0:T(8,128)(2,1)S(1)}, u32[]{:S(2)}, u32[]{:S(2)}) collective-permute-start(bf16[4,8,16,128]{3,2,1,0:T(8,128)(2,1)S(1)} %pad_maximum_fusion.1), channel_id=1, source_target_pairs={{0,6},{2,4},{4,2},{6,0},{8,14},{10,12},{12,10},{14,8},{16,22},{18,... | collective-permute-start | bytes 393224 | tf_op jit(solution)/shard_map/ppermute | solution.py:113
  18.4 3.6 %collective-permute-done.3 = bf16[4,8,16,128]{3,2,1,0:T(8,128)(2,1)S(1)} collective-permute-done((bf16[4,8,16,128]{3,2,1,0:T(8,128)(2,1)S(1)}, bf16[4,8,16,128]{3,2,1,0:T(8,128)(2,1)S(1)}, u32[]{:S(2)}, u32[]{:S(2)}) %collective-permute-start.3) | collective-permute-done | bytes 131104 | tf_op jit(solution)/shard_map/ppermute | solution.py:113
  22.0 0.0 copy-start
  22.0 0.3 %collective-permute-start.4 = (bf16[8,8,16,128]{3,2,1,0:T(8,128)(2,1)S(1)}, bf16[8,8,16,128]{3,2,1,0:T(8,128)(2,1)S(1)}, u32[]{:S(2)}, u32[]{:S(2)}) collective-permute-start(bf16[8,8,16,128]{3,2,1,0:T(8,128)(2,1)S(1)} %pad_maximum_fusion.refs_0_), channel_id=1, source_target_pairs={{0,2},{2,0},{4,6},{6,4},{8,10},{10,8},{12,14},{14,12},{16,18},{18,... | collective-permute-start | bytes 786440 | tf_op jit(solution)/shard_map/ppermute | solution.py:117
  22.3 1.3 %collective-permute-done.4.refs_1_ = bf16[8,8,16,128]{3,2,1,0:T(8,128)(2,1)S(1)} collective-permute-done((bf16[8,8,16,128]{3,2,1,0:T(8,128)(2,1)S(1)}, bf16[8,8,16,128]{3,2,1,0:T(8,128)(2,1)S(1)}, u32[]{:S(2)}, u32[]{:S(2)}) %collective-permute-start.4) | collective-permute-done | bytes 262176 | tf_op jit(solution)/shard_map/ppermute | solution.py:117
  23.6 0.0 copy-done
  23.6 0.0 copy-start.1
  23.6 0.7 %copy-done.1 = bf16[8,8,16,128]{3,2,1,0:T(8,128)(2,1)} copy-done((bf16[8,8,16,128]{3,2,1,0:T(8,128)(2,1)}, bf16[8,8,16,128]{3,2,1,0:T(8,128)(2,1)S(1)}, u32[]{:S(2)}) %copy-start.1) | copy-done | bytes 262168
  24.3 2.2 %shard_map.29 = f32[2,8,8,128]{3,2,1,0:T(8,128)} custom-call(bf16[8,8,16,128]{3,2,1,0:T(8,128)(2,1)} %copy-done, bf16[8,8,16,128]{3,2,1,0:T(8,128)(2,1)} %copy-done.1), custom_call_target="tpu_custom_call" | custom-call | tf_op jit(solution)/shard_map/pallas_call | solution.py:99
  (3 shorter events, 0.1 us)
Async XLA Ops:
  2.0 5.1 %collective-permute-start = (bf16[8,16,128]{2,1,0:T(8,128)(2,1)}, bf16[8,16,128]{2,1,0:T(8,128)(2,1)S(1)}, u32[]{:S(2)}, u32[]{:S(2)}) collective-permute-start(bf16[8,16,128]{2,1,0:T(8,128)(2,1)} %bitcast.9), channel_id=1, source_target_pairs={{0,1},{1,0},{2,3},{3,2},{4,5},{5,4},{6,7},{7,6},{8,9},{9,8},{10,11... | collective-permute-start | bytes 98312 | tf_op jit(solution)/shard_map/ppermute | solution.py:109
  8.0 4.3 %collective-permute-start.1 = (bf16[1,8,16,128]{3,2,1,0:T(8,128)(2,1)S(1)}, bf16[1,8,16,128]{3,2,1,0:T(8,128)(2,1)S(1)}, u32[]{:S(2)}, u32[]{:S(2)}) collective-permute-start(bf16[1,8,16,128]{3,2,1,0:T(8,128)(2,1)S(1)} %fusion), channel_id=1, source_target_pairs={{0,18},{2,16},{4,22},{6,20},{8,26},{10,24},{12,30},{14,28},{16,2},... | collective-permute-start | bytes 98312 | tf_op jit(solution)/shard_map/ppermute | solution.py:113
  12.3 4.2 %collective-permute-start.2 = (bf16[2,8,16,128]{3,2,1,0:T(8,128)(2,1)S(1)}, bf16[2,8,16,128]{3,2,1,0:T(8,128)(2,1)S(1)}, u32[]{:S(2)}, u32[]{:S(2)}) collective-permute-start(bf16[2,8,16,128]{3,2,1,0:T(8,128)(2,1)S(1)} %pad_maximum_fusion.2), channel_id=1, source_target_pairs={{0,10},{2,8},{4,14},{6,12},{8,2},{10,0},{12,6},{14,4},{16,26},{18,... | collective-permute-start | bytes 196616 | tf_op jit(solution)/shard_map/ppermute | solution.py:113
  16.5 5.5 %collective-permute-start.3 = (bf16[4,8,16,128]{3,2,1,0:T(8,128)(2,1)S(1)}, bf16[4,8,16,128]{3,2,1,0:T(8,128)(2,1)S(1)}, u32[]{:S(2)}, u32[]{:S(2)}) collective-permute-start(bf16[4,8,16,128]{3,2,1,0:T(8,128)(2,1)S(1)} %pad_maximum_fusion.1), channel_id=1, source_target_pairs={{0,6},{2,4},{4,2},{6,0},{8,14},{10,12},{12,10},{14,8},{16,22},{18,... | collective-permute-start | bytes 393224 | tf_op jit(solution)/shard_map/ppermute | solution.py:113
  22.0 1.6 %copy-start = (bf16[8,8,16,128]{3,2,1,0:T(8,128)(2,1)}, bf16[8,8,16,128]{3,2,1,0:T(8,128)(2,1)S(1)}, u32[]{:S(2)}) copy-start(bf16[8,8,16,128]{3,2,1,0:T(8,128)(2,1)S(1)} %pad_maximum_fusion.refs_0_) | copy-start | bytes 786436
  22.0 1.6 %collective-permute-start.4 = (bf16[8,8,16,128]{3,2,1,0:T(8,128)(2,1)S(1)}, bf16[8,8,16,128]{3,2,1,0:T(8,128)(2,1)S(1)}, u32[]{:S(2)}, u32[]{:S(2)}) collective-permute-start(bf16[8,8,16,128]{3,2,1,0:T(8,128)(2,1)S(1)} %pad_maximum_fusion.refs_0_), channel_id=1, source_target_pairs={{0,2},{2,0},{4,6},{6,4},{8,10},{10,8},{12,14},{14,12},{16,18},{18,... | collective-permute-start | bytes 786440 | tf_op jit(solution)/shard_map/ppermute | solution.py:117
  23.6 0.7 %copy-start.1 = (bf16[8,8,16,128]{3,2,1,0:T(8,128)(2,1)}, bf16[8,8,16,128]{3,2,1,0:T(8,128)(2,1)S(1)}, u32[]{:S(2)}) copy-start(bf16[8,8,16,128]{3,2,1,0:T(8,128)(2,1)S(1)} %collective-permute-done.4.refs_1_) | copy-start | bytes 786436

commit v2 on v1

--- a/solution.py
+++ b/solution.py
@@ -8,29 +8,42 @@
 from jax.sharding import PartitionSpec as P
 
 
-def beam_kernel(parts, v_ref, w_ref, mine_ref, send_ref, w32, both):
+def room_for(*arrays):
+    return (4 << 20) + 4 * sum(a.size * a.dtype.itemsize for a in arrays)
+
+
+def beam_kernel(parts, v_ref, w_ref, mine_ref, copy_ref, send_ref, w16, w32, volts, both, sems):
     planes, elems, chans, samples = v_ref.shape
     rows = w_ref.shape[0] // chans
     deep = elems * chans
-    w32[...] = w_ref[...].astype(jnp.float32)
-    by_channel = jnp.concatenate([w32[pl.ds(c, rows, stride=chans), :] for c in range(chans)])
+    loads = [pltpu.make_async_copy(w_ref, w16, sems.at[planes])]
+    loads += [pltpu.make_async_copy(v_ref.at[p], volts.at[p], sems.at[p]) for p in range(planes)]
+    for load in loads:
+        load.start()
     lane = lax.broadcasted_iota(jnp.int32, (elems, deep), 1)
     low = lax.broadcasted_iota(jnp.int32, (elems, deep), 0) * chans
     spread = jnp.where((lane >= low) & (lane < low + chans), 1.0, 0.0).astype(jnp.bfloat16)
+    loads[0].wait()
+    w32[...] = w16[...].astype(jnp.float32)
+    by_channel = jnp.concatenate([w32[pl.ds(c, rows, stride=chans), :] for c in range(chans)])
     wide = jnp.dot(by_channel.astype(jnp.bfloat16), spread, preferred_element_type=jnp.float32)
     wide = wide.reshape(chans, rows, deep)
     lane = lax.rem(lax.broadcasted_iota(jnp.int32, wide.shape, 2), chans)
     wide = jnp.where(lane == lax.broadcasted_iota(jnp.int32, wide.shape, 0), wide, 0.0)
     wide = wide.reshape(chans * rows, deep).astype(jnp.bfloat16)
-    volts = v_ref[...].reshape(planes, deep, samples)
     half = rows // 2
-    by_real = jnp.dot(wide, volts[0], preferred_element_type=jnp.float32).reshape(chans, 2, half, samples)
-    by_imag = jnp.dot(wide, volts[1], preferred_element_type=jnp.float32).reshape(chans, 2, half, samples)
+    loads[1].wait()
+    by_real = jnp.dot(wide, volts[0].reshape(deep, samples), preferred_element_type=jnp.float32)
+    by_real = by_real.reshape(chans, 2, half, samples)
+    loads[2].wait()
+    by_imag = jnp.dot(wide, volts[1].reshape(deep, samples), preferred_element_type=jnp.float32)
+    by_imag = by_imag.reshape(chans, 2, half, samples)
     both[:, 0] = by_real[:, 0] + by_imag[:, 1]
     both[:, 1] = by_imag[:, 0] - by_real[:, 1]
     owned = chans // parts
     me = lax.axis_index("elem")
     mine_ref[...] = both[pl.ds(me * owned, owned)].reshape(mine_ref.shape)
+    copy_ref[...] = mine_ref[...].astype(jnp.bfloat16)
     for step in range(1, parts):
         other = lax.rem(me + step, parts) * owned
         send_ref[step - 1] = both[pl.ds(other, owned)].reshape(mine_ref.shape).astype(jnp.bfloat16)
@@ -42,13 +55,20 @@
     owned = chans // parts
     return pl.pallas_call(
         functools.partial(beam_kernel, parts),
+        in_specs=[pl.BlockSpec(memory_space=pltpu.HBM)] * 2,
         out_shape=(
             jax.ShapeDtypeStruct((owned, rows, samples), jnp.float32),
+            jax.ShapeDtypeStruct((owned, rows, samples), jnp.bfloat16),
             jax.ShapeDtypeStruct((parts - 1, owned, rows, samples), jnp.bfloat16),
         ),
+        out_specs=[pl.BlockSpec(memory_space=pltpu.VMEM)] * 3,
+        compiler_params=pltpu.CompilerParams(vmem_limit_bytes=55080 << 10),
         scratch_shapes=[
+            pltpu.VMEM((rows * chans, elems), weights.dtype),
             pltpu.VMEM((rows * chans, elems), jnp.float32),
+            pltpu.VMEM((planes, elems, chans, samples), voltages.dtype),
             pltpu.VMEM((chans, planes, rows // planes, samples), jnp.float32),
+            pltpu.SemaphoreType.DMA((planes + 1,)),
         ],
     )(voltages[:, 0], weights.transpose(0, 1, 3, 2).reshape(rows * chans, elems))
 
@@ -99,36 +119,44 @@
     return pl.pallas_call(
         functools.partial(spectra_kernel, order),
         out_shape=jax.ShapeDtypeStruct((2, chans, rows // 2, stations * (rows // 2)), jnp.float32),
+        compiler_params=pltpu.CompilerParams(vmem_limit_bytes=room_for(*blocks)),
     )(*blocks)
 
 
-def body(steps, stations, parts, voltages, weights):
-    mine, sent = partial_beams(voltages, weights, parts)
+def gather_plan(stations):
+    bits = []
+    while stations > 2:
+        stations //= 2
+        bits.append(stations)
+    first, rest = bits[0], bits[1:]
+    stages = []
+    while rest:
+        pair, rest = rest[:2], rest[2:]
+        stages.append([b + 1 for b in pair] + ([sum(pair) + 1] if len(pair) == 2 else []))
+    return first + 1, stages + [[1]]
+
+
+def body(stations, parts, voltages, weights):
+    mine, copy, sent = partial_beams(voltages, weights, parts)
+    near, stages = gather_plan(stations)
+    other = lax.ppermute(copy, "stn", [(i, i ^ near) for i in range(stations)]).astype(jnp.float32)
     for step in range(1, parts):
-        pairs = [(i, (i + step) % parts) for i in range(parts)]
-        mine = mine + lax.ppermute(sent[step - 1], "elem", pairs).astype(jnp.float32)
-    held = mine.astype(jnp.bfloat16)[None]
-    offsets = [0]
-    for step in steps[:-1]:
-        got = lax.ppermute(held, "stn", [(i, i ^ step) for i in range(stations)])
-        held = jnp.concatenate([held, got])
-        offsets += [o ^ step for o in offsets]
-    step = steps[-1]
-    got = lax.ppermute(held, "stn", [(i, i ^ step) for i in range(stations)])
-    offsets += [o ^ step for o in offsets]
-    return cross_spectra([held, got], offsets)
+        here = [(e, (e + step) % parts) for e in range(parts)]
+        there = [(s * parts + e, (s ^ near) * parts + f) for s in range(stations) for e, f in here]
+        mine = mine + lax.ppermute(sent[step - 1], "elem", here).astype(jnp.float32)
+        other = other + lax.ppermute(sent[step - 1], ("stn", "elem"), there).astype(jnp.float32)
+    held, offsets = jnp.stack([mine, other]).astype(jnp.bfloat16), [0, near]
+    for steps in stages:
+        got = [lax.ppermute(held, "stn", [(i, i ^ step) for i in range(stations)]) for step in steps]
+        offsets = offsets + [o ^ step for step in steps for o in offsets]
+        if steps is not stages[-1]:
+            held = jnp.concatenate([held] + got)
+    return cross_spectra([held] + got, offsets)
 
 
 def solution(mesh):
-    stations, parts = mesh.shape["stn"], mesh.shape["elem"]
-    steps = []
-    bit = stations // 2
-    while bit > 1:
-        steps.append(bit + 1)
-        bit //= 2
-    steps.append(1)
     placed = (P(None, "stn", "elem", None, None), P(None, None, "elem", None))
     return jax.shard_map(
-        functools.partial(body, steps, stations, parts),
+        functools.partial(body, mesh.shape["stn"], mesh.shape["elem"]),
         mesh=mesh, in_specs=placed, out_specs=P(None, "elem", "stn", None), check_vma=False,
     )

time: 26.7 us -> 21.5 us (0.81)
  waiting for transfers between devices: 12 us -> 8.29 us
  starting transfers between devices: 8.64 us -> 10.3 us
  Pallas kernels: 4.24 us -> 2.73 us
  other arithmetic: 0.9 us -> 0.05 us
  local copies, waits for them, and re-layouts: 0.7 us -> 0.04 us
    ppermute x5 -> x7, waiting for transfers between devices: 12 us -> 8.29 us  [the longest x4 4.54 us: body(): lax.ppermute(held, 'stn', [(i, i ^ step) for i in range(stations)])]
    ppermute x5 -> x7, starting transfers between devices: 8.64 us -> 10.3 us  [the longest x4 5.06 us: body(): lax.ppermute(held, 'stn', [(i, i ^ step) for i in range(stations)])]
    pallas_call x1, Pallas kernels: 2.2 us -> 1.18 us  [cross_spectra(): pl.pallas_call(functools.partial(spectra_kernel, order), out_shape=jax.Sh...]
    broadcast_in_dim x1 -> x0, other arithmetic: 0.85 us -> none  [body(): held = mine.astype(jnp.bfloat16)[None]]
    unnamed x4 -> x2, local copies, waits for them, and re-layouts: 0.7 us -> 0.03 us
    pallas_call x1, Pallas kernels: 2.04 us -> 1.55 us  [partial_beams(): pl.pallas_call(functools.partial(beam_kernel, parts), in_specs=[pl.BlockS...]
  transfers between devices with their start and end apart: 5 -> 7, of which waited for: 5 -> 6; matrix products, arithmetic and copies ran while one was open for 0% -> 0% of each run, Pallas kernels for 0% -> 0%
where the time goes in v2:
time: 21.5 us; the launch traced here: 21.4 us
  starting transfers between devices  10.3 us (48%)
  waiting for transfers between devices  8.29 us (39%)
  Pallas kernels  2.73 us (13%)
    ppermute x4, starting transfers between devices, body(): lax.ppermute(held, 'stn', [(i, i ^ step) for i in range(stations)])  5.06 us
    ppermute x4, waiting for transfers between devices, body(): lax.ppermute(held, 'stn', [(i, i ^ step) for i in range(stations)])  4.54 us
    ppermute x1, waiting for transfers between devices, body(): lax.ppermute(sent[step - 1], ('stn', 'elem'), there).astype(jnp.float32)  3.05 us
    ppermute x1, starting transfers between devices, body(): mine = mine + lax.ppermute(sent[step - 1], 'elem', here).astype(jnp.float32)  3.03 us
    ppermute x1, starting transfers between devices, body(): lax.ppermute(sent[step - 1], ('stn', 'elem'), there).astype(jnp.float32)  1.69 us
    pallas_call x1, Pallas kernels, partial_beams(): pl.pallas_call(functools.partial(beam_kernel, parts), in_specs=[pl.BlockS...  1.55 us
    pallas_call x1, Pallas kernels, cross_spectra(): pl.pallas_call(functools.partial(spectra_kernel, order), out_shape=jax.Sh...  1.18 us
    ppermute x1, waiting for transfers between devices, body(): lax.ppermute(copy, 'stn', [(i, i ^ near) for i in range(stations)])  0.7 us
  transfers between devices with their start and end apart: 7, of which 6 were waited for; matrix products, arithmetic and copies ran while one was open for 0% of the time, Pallas kernels for 0%

profile of v2, /device:TPU:0, one launch (start us, length us, event | category | flops | bytes accessed | tf_op | source)
XLA Modules:
  0.0 21.4 jit_solution(2356609159178631701)
XLA Ops:
  0.0 1.5 %shard_map.28 = (f32[8,16,128]{2,1,0:T(8,128)S(1)}, bf16[8,16,128]{2,1,0:T(8,128)(2,1)S(1)}, bf16[1,8,16,128]{3,2,1,0:T(8,128)(2,1)S(1)}) custom-call(bf16[2,32,16,128]{3,2,1,0:T(8,128)(2,1)} %bitcast.13, bf16[256,32]{1,0:T(8,128)(2,1)} %bitcast.14), custom_call_target="tpu_custom_call" | custom-call | tf_op jit(solution)/shard_map/pallas_call | solution.py:56
  1.6 3.0 %collective-permute-start = (bf16[8,16,128]{2,1,0:T(8,128)(2,1)S(1)}, bf16[8,16,128]{2,1,0:T(8,128)(2,1)S(1)}, u32[]{:S(2)}, u32[]{:S(2)}) collective-permute-start(bf16[8,16,128]{2,1,0:T(8,128)(2,1)S(1)} %bitcast.11), channel_id=1, source_target_pairs={{0,1},{1,0},{2,3},{3,2},{4,5},{5,4},{6,7},{7,6},{8,9},{9,8},{10,11... | collective-permute-start | bytes 98312 | tf_op jit(solution)/shard_map/ppermute | solution.py:146
  4.6 1.7 %collective-permute-start.2 = (bf16[8,16,128]{2,1,0:T(8,128)(2,1)S(1)}, bf16[8,16,128]{2,1,0:T(8,128)(2,1)S(1)}, u32[]{:S(2)}, u32[]{:S(2)}) collective-permute-start(bf16[8,16,128]{2,1,0:T(8,128)(2,1)S(1)} %bitcast.12), channel_id=1, source_target_pairs={{0,19},{1,18},{2,17},{3,16},{4,23},{5,22},{6,21},{7,20},{8,27},{9,... | collective-permute-start | bytes 98312 | tf_op jit(solution)/shard_map/ppermute | solution.py:147
  6.3 0.5 %collective-permute-start.1 = (bf16[8,16,128]{2,1,0:T(8,128)(2,1)S(1)}, bf16[8,16,128]{2,1,0:T(8,128)(2,1)S(1)}, u32[]{:S(2)}, u32[]{:S(2)}) collective-permute-start(bf16[8,16,128]{2,1,0:T(8,128)(2,1)S(1)} %get-tuple-element.10), channel_id=1, source_target_pairs={{0,18},{2,16},{4,22},{6,20},{8,26},{10,24},{12,30},{14,28},{16,2},... | collective-permute-start | bytes 98312 | tf_op jit(solution)/shard_map/ppermute | solution.py:142
  6.8 0.0 collective-permute-done
  6.8 3.0 %collective-permute-done.2 = bf16[8,16,128]{2,1,0:T(8,128)(2,1)S(1)} collective-permute-done((bf16[8,16,128]{2,1,0:T(8,128)(2,1)S(1)}, bf16[8,16,128]{2,1,0:T(8,128)(2,1)S(1)}, u32[]{:S(2)}, u32[]{:S(2)}) %collective-permute-start.2) | collective-permute-done | bytes 32800 | tf_op jit(solution)/shard_map/ppermute | solution.py:147
  9.8 0.7 %collective-permute-done.1 = bf16[8,16,128]{2,1,0:T(8,128)(2,1)S(1)} collective-permute-done((bf16[8,16,128]{2,1,0:T(8,128)(2,1)S(1)}, bf16[8,16,128]{2,1,0:T(8,128)(2,1)S(1)}, u32[]{:S(2)}, u32[]{:S(2)}) %collective-permute-start.1) | collective-permute-done | bytes 32800 | tf_op jit(solution)/shard_map/ppermute | solution.py:142
  10.6 2.2 %collective-permute-start.3 = (bf16[2,8,16,128]{3,2,1,0:T(8,128)(2,1)S(1)}, bf16[2,8,16,128]{3,2,1,0:T(8,128)(2,1)S(1)}, u32[]{:S(2)}, u32[]{:S(2)}) collective-permute-start(bf16[2,8,16,128]{3,2,1,0:T(8,128)(2,1)S(1)} %pad_maximum_fusion), channel_id=1, source_target_pairs={{0,10},{2,8},{4,14},{6,12},{8,2},{10,0},{12,6},{14,4},{16,26},{18,... | collective-permute-start | bytes 196616 | tf_op jit(solution)/shard_map/ppermute | solution.py:150
  12.8 0.7 %collective-permute-start.4 = (bf16[2,8,16,128]{3,2,1,0:T(8,128)(2,1)S(1)}, bf16[2,8,16,128]{3,2,1,0:T(8,128)(2,1)S(1)}, u32[]{:S(2)}, u32[]{:S(2)}) collective-permute-start(bf16[2,8,16,128]{3,2,1,0:T(8,128)(2,1)S(1)} %pad_maximum_fusion), channel_id=1, source_target_pairs={{0,6},{2,4},{4,2},{6,0},{8,14},{10,12},{12,10},{14,8},{16,22},{18,... | collective-permute-start | bytes 196616 | tf_op jit(solution)/shard_map/ppermute | solution.py:150
  13.4 1.2 %collective-permute-start.5 = (bf16[2,8,16,128]{3,2,1,0:T(8,128)(2,1)S(1)}, bf16[2,8,16,128]{3,2,1,0:T(8,128)(2,1)S(1)}, u32[]{:S(2)}, u32[]{:S(2)}) collective-permute-start(bf16[2,8,16,128]{3,2,1,0:T(8,128)(2,1)S(1)} %pad_maximum_fusion), channel_id=1, source_target_pairs={{0,14},{2,12},{4,10},{6,8},{8,6},{10,4},{12,2},{14,0},{16,30},{18,... | collective-permute-start | bytes 196616 | tf_op jit(solution)/shard_map/ppermute | solution.py:150
  14.6 0.1 collective-permute-done.3
  14.7 2.4 %collective-permute-done.4 = bf16[2,8,16,128]{3,2,1,0:T(8,128)(2,1)S(1)} collective-permute-done((bf16[2,8,16,128]{3,2,1,0:T(8,128)(2,1)S(1)}, bf16[2,8,16,128]{3,2,1,0:T(8,128)(2,1)S(1)}, u32[]{:S(2)}, u32[]{:S(2)}) %collective-permute-start.4) | collective-permute-done | bytes 65568 | tf_op jit(solution)/shard_map/ppermute | solution.py:150
  17.1 0.9 %collective-permute-done.5 = bf16[2,8,16,128]{3,2,1,0:T(8,128)(2,1)S(1)} collective-permute-done((bf16[2,8,16,128]{3,2,1,0:T(8,128)(2,1)S(1)}, bf16[2,8,16,128]{3,2,1,0:T(8,128)(2,1)S(1)}, u32[]{:S(2)}, u32[]{:S(2)}) %collective-permute-start.5) | collective-permute-done | bytes 65568 | tf_op jit(solution)/shard_map/ppermute | solution.py:150
  18.0 1.0 %collective-permute-start.6 = (bf16[8,8,16,128]{3,2,1,0:T(8,128)(2,1)S(1)}, bf16[8,8,16,128]{3,2,1,0:T(8,128)(2,1)S(1)}, u32[]{:S(2)}, u32[]{:S(2)}) collective-permute-start(bf16[8,8,16,128]{3,2,1,0:T(8,128)(2,1)S(1)} %constant_dynamic-update-slice_fusion.refs_0_), channel_id=1, source_target_pairs={{0,2},{2,0},{4,6},{6,4},{8,10},{10,8},{12,14},{14,12},{16,18},{18,... | collective-permute-start | bytes 786440 | tf_op jit(solution)/shard_map/ppermute | solution.py:150
  19.0 1.2 %collective-permute-done.6.refs_1_ = bf16[8,8,16,128]{3,2,1,0:T(8,128)(2,1)S(1)} collective-permute-done((bf16[8,8,16,128]{3,2,1,0:T(8,128)(2,1)S(1)}, bf16[8,8,16,128]{3,2,1,0:T(8,128)(2,1)S(1)}, u32[]{:S(2)}, u32[]{:S(2)}) %collective-permute-start.6) | collective-permute-done | bytes 262176 | tf_op jit(solution)/shard_map/ppermute | solution.py:150
  20.2 1.2 %shard_map.29 = f32[2,8,8,128]{3,2,1,0:T(8,128)} custom-call(bf16[8,8,16,128]{3,2,1,0:T(8,128)(2,1)S(1)} %constant_dynamic-update-slice_fusion.refs_0_, bf16[8,8,16,128]{3,2,1,0:T(8,128)(2,1)S(1)} %collective-permute-done.6.refs_1_), custom_call_target="tpu_custom_call" | custom-call | tf_op jit(solution)/shard_map/pallas_call | solution.py:119
  (6 shorter events, 0.1 us)
Async XLA Ops:
  1.6 5.2 %collective-permute-start = (bf16[8,16,128]{2,1,0:T(8,128)(2,1)S(1)}, bf16[8,16,128]{2,1,0:T(8,128)(2,1)S(1)}, u32[]{:S(2)}, u32[]{:S(2)}) collective-permute-start(bf16[8,16,128]{2,1,0:T(8,128)(2,1)S(1)} %bitcast.11), channel_id=1, source_target_pairs={{0,1},{1,0},{2,3},{3,2},{4,5},{5,4},{6,7},{7,6},{8,9},{9,8},{10,11... | collective-permute-start | bytes 98312 | tf_op jit(solution)/shard_map/ppermute | solution.py:146
  4.6 5.2 %collective-permute-start.2 = (bf16[8,16,128]{2,1,0:T(8,128)(2,1)S(1)}, bf16[8,16,128]{2,1,0:T(8,128)(2,1)S(1)}, u32[]{:S(2)}, u32[]{:S(2)}) collective-permute-start(bf16[8,16,128]{2,1,0:T(8,128)(2,1)S(1)} %bitcast.12), channel_id=1, source_target_pairs={{0,19},{1,18},{2,17},{3,16},{4,23},{5,22},{6,21},{7,20},{8,27},{9,... | collective-permute-start | bytes 98312 | tf_op jit(solution)/shard_map/ppermute | solution.py:147
  6.3 4.2 %collective-permute-start.1 = (bf16[8,16,128]{2,1,0:T(8,128)(2,1)S(1)}, bf16[8,16,128]{2,1,0:T(8,128)(2,1)S(1)}, u32[]{:S(2)}, u32[]{:S(2)}) collective-permute-start(bf16[8,16,128]{2,1,0:T(8,128)(2,1)S(1)} %get-tuple-element.10), channel_id=1, source_target_pairs={{0,18},{2,16},{4,22},{6,20},{8,26},{10,24},{12,30},{14,28},{16,2},... | collective-permute-start | bytes 98312 | tf_op jit(solution)/shard_map/ppermute | solution.py:142
  10.6 4.1 %collective-permute-start.3 = (bf16[2,8,16,128]{3,2,1,0:T(8,128)(2,1)S(1)}, bf16[2,8,16,128]{3,2,1,0:T(8,128)(2,1)S(1)}, u32[]{:S(2)}, u32[]{:S(2)}) collective-permute-start(bf16[2,8,16,128]{3,2,1,0:T(8,128)(2,1)S(1)} %pad_maximum_fusion), channel_id=1, source_target_pairs={{0,10},{2,8},{4,14},{6,12},{8,2},{10,0},{12,6},{14,4},{16,26},{18,... | collective-permute-start | bytes 196616 | tf_op jit(solution)/shard_map/ppermute | solution.py:150
  12.8 4.3 %collective-permute-start.4 = (bf16[2,8,16,128]{3,2,1,0:T(8,128)(2,1)S(1)}, bf16[2,8,16,128]{3,2,1,0:T(8,128)(2,1)S(1)}, u32[]{:S(2)}, u32[]{:S(2)}) collective-permute-start(bf16[2,8,16,128]{3,2,1,0:T(8,128)(2,1)S(1)} %pad_maximum_fusion), channel_id=1, source_target_pairs={{0,6},{2,4},{4,2},{6,0},{8,14},{10,12},{12,10},{14,8},{16,22},{18,... | collective-permute-start | bytes 196616 | tf_op jit(solution)/shard_map/ppermute | solution.py:150
  13.4 4.6 %collective-permute-start.5 = (bf16[2,8,16,128]{3,2,1,0:T(8,128)(2,1)S(1)}, bf16[2,8,16,128]{3,2,1,0:T(8,128)(2,1)S(1)}, u32[]{:S(2)}, u32[]{:S(2)}) collective-permute-start(bf16[2,8,16,128]{3,2,1,0:T(8,128)(2,1)S(1)} %pad_maximum_fusion), channel_id=1, source_target_pairs={{0,14},{2,12},{4,10},{6,8},{8,6},{10,4},{12,2},{14,0},{16,30},{18,... | collective-permute-start | bytes 196616 | tf_op jit(solution)/shard_map/ppermute | solution.py:150
  18.0 2.2 %collective-permute-start.6 = (bf16[8,8,16,128]{3,2,1,0:T(8,128)(2,1)S(1)}, bf16[8,8,16,128]{3,2,1,0:T(8,128)(2,1)S(1)}, u32[]{:S(2)}, u32[]{:S(2)}) collective-permute-start(bf16[8,8,16,128]{3,2,1,0:T(8,128)(2,1)S(1)} %constant_dynamic-update-slice_fusion.refs_0_), channel_id=1, source_target_pairs={{0,2},{2,0},{4,6},{6,4},{8,10},{10,8},{12,14},{14,12},{16,18},{18,... | collective-permute-start | bytes 786440 | tf_op jit(solution)/shard_map/ppermute | solution.py:150

commit v3 on v2

--- a/solution.py
+++ b/solution.py
@@ -73,54 +73,61 @@
     )(voltages[:, 0], weights.transpose(0, 1, 3, 2).reshape(rows * chans, elems))
 
 
-def spectra_kernel(order, *refs):
-    blocks, out_ref = refs[:-1], refs[-1]
-    chans, rows, samples = blocks[0].shape[1:]
+def place_of(chip, stages):
+    index, flip, size = 0, 0, 1
+    for steps in stages:
+        bits = [s >> 1 for s in steps if (s >> 1) & ((s >> 1) - 1) == 0]
+        spots, flips = 0, 0
+        for at, step in enumerate(steps):
+            key = sum(1 << j for j, b in enumerate(bits) if (step >> 1) & b)
+            spots |= (at + 1) << (2 * key)
+            flips |= (step & 1) << key
+        key = sum(((chip >> (b.bit_length() - 1)) & 1) << j for j, b in enumerate(bits))
+        index = index + ((spots >> (2 * key)) & 3) * size
+        flip = flip ^ ((flips >> key) & 1)
+        size *= len(steps) + 1
+    return index, flip
+
+
+def spectra_kernel(stages, held_ref, got_ref, out_ref):
+    chips, chans, rows, samples = held_ref.shape
     half = rows // 2
-    where = [(ref, i) for ref in blocks for i in range(ref.shape[0])]
     me = lax.axis_index("stn")
+    places = []
+    for chip in range(chips):
+        index, flip = place_of((me >> 1) ^ chip, stages)
+        places.append((index, ((me & 1) ^ flip) == 0))
     found = []
     for c in range(chans):
-        tiles = [where[k][0][where[k][1], c].astype(jnp.float32) for k in order]
-        real = jnp.concatenate([t[:half] for t in tiles]).astype(jnp.bfloat16)
-        imag = jnp.concatenate([t[half:] for t in tiles]).astype(jnp.bfloat16)
-        own = tiles[0]
+        tiles = []
+        for index, held_first in places:
+            held, got = held_ref[index, c], got_ref[index, c]
+            tiles += [jnp.where(held_first, held, got), jnp.where(held_first, got, held)]
+        tiles = [t.astype(jnp.float32) for t in tiles]
+        real = jnp.concatenate([t[:half] for t in tiles])
+        imag = jnp.concatenate([t[half:] for t in tiles])
+        own = held_ref[0, c].astype(jnp.float32)
         left = jnp.concatenate([own, jnp.concatenate([own[half:], -own[:half]])], axis=1)
         right = jnp.concatenate([real, imag], axis=1)
         found.append(
             lax.dot_general(
-                left.astype(jnp.bfloat16), right, (((1,), (1,)), ((), ())),
+                left.astype(jnp.bfloat16), right.astype(jnp.bfloat16), (((1,), (1,)), ((), ())),
                 preferred_element_type=jnp.float32,
             )
         )
-    spec = jnp.concatenate(found)
-    beams = spec.shape[1]
-    lane = lax.broadcasted_iota(jnp.int32, spec.shape, 1)
-    bit, width = 1, half
-    while width < beams:
-        if width < 128:
-            moved = jnp.where(
-                lane & width == 0, pltpu.roll(spec, beams - width, 1), pltpu.roll(spec, width, 1)
-            )
-        else:
-            cuts = [spec[:, at : at + width] for at in range(0, beams, width)]
-            moved = jnp.concatenate([cuts[i ^ 1] for i in range(len(cuts))], axis=1)
-        spec = jnp.where(me & bit != 0, moved, spec)
-        bit, width = bit * 2, width * 2
-    spec = spec.reshape(chans, 2, half, beams) / jnp.float32(samples)
+    spec = jnp.concatenate(found).reshape(chans, 2, half, -1) / jnp.float32(samples)
     out_ref[0] = spec[:, 0]
     out_ref[1] = spec[:, 1]
 
 
-def cross_spectra(blocks, offsets):
-    chans, rows, samples = blocks[0].shape[1:]
-    stations = len(offsets)
-    order = [offsets.index(d) for d in range(stations)]
+def cross_spectra(held, got, stages):
+    chips, chans, rows, samples = held.shape
+    half = rows // 2
     return pl.pallas_call(
-        functools.partial(spectra_kernel, order),
-        out_shape=jax.ShapeDtypeStruct((2, chans, rows // 2, stations * (rows // 2)), jnp.float32),
-        compiler_params=pltpu.CompilerParams(vmem_limit_bytes=room_for(*blocks)),
-    )(*blocks)
+        functools.partial(spectra_kernel, stages),
+        out_shape=jax.ShapeDtypeStruct((2, chans, half, 2 * chips * half), jnp.float32),
+        compiler_params=pltpu.CompilerParams(vmem_limit_bytes=room_for(held, got)),
+    )(held, got)
 
 
 def gather_plan(stations):
@@ -132,8 +139,8 @@
     stages = []
     while rest:
         pair, rest = rest[:2], rest[2:]
-        stages.append([b + 1 for b in pair] + ([sum(pair) + 1] if len(pair) == 2 else []))
-    return first + 1, stages + [[1]]
+        stages.append([sum(pair), pair[0], pair[1] + 1] if len(pair) == 2 else [pair[0] + 1])
+    return first + 1, stages
 
 
 def body(stations, parts, voltages, weights):
@@ -145,13 +152,12 @@
         there = [(s * parts + e, (s ^ near) * parts + f) for s in range(stations) for e, f in here]
         mine = mine + lax.ppermute(sent[step - 1], "elem", here).astype(jnp.float32)
         other = other + lax.ppermute(sent[step - 1], ("stn", "elem"), there).astype(jnp.float32)
-    held, offsets = jnp.stack([mine, other]).astype(jnp.bfloat16), [0, near]
+    held = jnp.stack([mine, other]).astype(jnp.bfloat16)
     for steps in stages:
         got = [lax.ppermute(held, "stn", [(i, i ^ step) for i in range(stations)]) for step in steps]
-        offsets = offsets + [o ^ step for step in steps for o in offsets]
-        if steps is not stages[-1]:
-            held = jnp.concatenate([held] + got)
-    return cross_spectra([held] + got, offsets)
+        held = jnp.concatenate([held] + got)
+    got = lax.ppermute(held, "stn", [(i, i ^ 1) for i in range(stations)])
+    return cross_spectra(held, got, [[near]] + stages)
 
 
 def solution(mesh):

time: 21.5 us -> 20.6 us (0.958)
  starting transfers between devices: 10.3 us -> 9.12 us
  waiting for transfers between devices: 8.29 us -> 8.78 us
  Pallas kernels: 2.73 us -> 2.46 us
    ppermute x0 -> x1, waiting for transfers between devices: none -> 1.45 us  [body(): got = lax.ppermute(held, 'stn', [(i, i ^ 1) for i in range(stations)])]
    ppermute x4 -> x3, starting transfers between devices: 5.06 us -> 3.77 us  [body(): lax.ppermute(held, 'stn', [(i, i ^ step) for i in range(stations)])]
    ppermute x4 -> x3, waiting for transfers between devices: 4.54 us -> 3.58 us  [body(): lax.ppermute(held, 'stn', [(i, i ^ step) for i in range(stations)])]
    pallas_call x1, Pallas kernels: 1.18 us -> 0.91 us  [cross_spectra(): pl.pallas_call(functools.partial(spectra_kernel, stages), out_shape=jax.S...]
  transfers between devices with their start and end apart: 7 -> 7, of which waited for: 6 -> 5; matrix products, arithmetic and copies ran while one was open for 0% -> 0% of each run, Pallas kernels for 0% -> 0%
where the time goes in v3:
time: 20.6 us; the launch traced here: 20.5 us
  starting transfers between devices  9.12 us (44%)
  waiting for transfers between devices  8.78 us (43%)
  Pallas kernels  2.46 us (12%)
    ppermute x3, starting transfers between devices, body(): lax.ppermute(held, 'stn', [(i, i ^ step) for i in range(stations)])  3.77 us
    ppermute x3, waiting for transfers between devices, body(): lax.ppermute(held, 'stn', [(i, i ^ step) for i in range(stations)])  3.58 us
    ppermute x1, waiting for transfers between devices, body(): lax.ppermute(sent[step - 1], ('stn', 'elem'), there).astype(jnp.float32)  3.05 us
    ppermute x1, starting transfers between devices, body(): mine = mine + lax.ppermute(sent[step - 1], 'elem', here).astype(jnp.float32)  3.03 us
    ppermute x1, starting transfers between devices, body(): lax.ppermute(sent[step - 1], ('stn', 'elem'), there).astype(jnp.float32)  1.69 us
    pallas_call x1, Pallas kernels, partial_beams(): pl.pallas_call(functools.partial(beam_kernel, parts), in_specs=[pl.BlockS...  1.55 us
    ppermute x1, waiting for transfers between devices, body(): got = lax.ppermute(held, 'stn', [(i, i ^ 1) for i in range(stations)])  1.45 us
    pallas_call x1, Pallas kernels, cross_spectra(): pl.pallas_call(functools.partial(spectra_kernel, stages), out_shape=jax.S...  0.91 us
  transfers between devices with their start and end apart: 7, of which 5 were waited for; matrix products, arithmetic and copies ran while one was open for 0% of the time, Pallas kernels for 0%

profile of v3, /device:TPU:0, one launch (start us, length us, event | category | flops | bytes accessed | tf_op | source)
XLA Modules:
  0.0 20.5 jit_solution(314945266764844603)
XLA Ops:
  0.0 1.5 %shard_map.28 = (f32[8,16,128]{2,1,0:T(8,128)S(1)}, bf16[8,16,128]{2,1,0:T(8,128)(2,1)S(1)}, bf16[1,8,16,128]{3,2,1,0:T(8,128)(2,1)S(1)}) custom-call(bf16[2,32,16,128]{3,2,1,0:T(8,128)(2,1)} %bitcast.13, bf16[256,32]{1,0:T(8,128)(2,1)} %bitcast.14), custom_call_target="tpu_custom_call" | custom-call | tf_op jit(solution)/shard_map/pallas_call | solution.py:56
  1.6 3.0 %collective-permute-start = (bf16[8,16,128]{2,1,0:T(8,128)(2,1)S(1)}, bf16[8,16,128]{2,1,0:T(8,128)(2,1)S(1)}, u32[]{:S(2)}, u32[]{:S(2)}) collective-permute-start(bf16[8,16,128]{2,1,0:T(8,128)(2,1)S(1)} %bitcast.11), channel_id=1, source_target_pairs={{0,1},{1,0},{2,3},{3,2},{4,5},{5,4},{6,7},{7,6},{8,9},{9,8},{10,11... | collective-permute-start | bytes 98312 | tf_op jit(solution)/shard_map/ppermute | solution.py:153
  4.6 1.7 %collective-permute-start.2 = (bf16[8,16,128]{2,1,0:T(8,128)(2,1)S(1)}, bf16[8,16,128]{2,1,0:T(8,128)(2,1)S(1)}, u32[]{:S(2)}, u32[]{:S(2)}) collective-permute-start(bf16[8,16,128]{2,1,0:T(8,128)(2,1)S(1)} %bitcast.12), channel_id=1, source_target_pairs={{0,19},{1,18},{2,17},{3,16},{4,23},{5,22},{6,21},{7,20},{8,27},{9,... | collective-permute-start | bytes 98312 | tf_op jit(solution)/shard_map/ppermute | solution.py:154
  6.3 0.5 %collective-permute-start.1 = (bf16[8,16,128]{2,1,0:T(8,128)(2,1)S(1)}, bf16[8,16,128]{2,1,0:T(8,128)(2,1)S(1)}, u32[]{:S(2)}, u32[]{:S(2)}) collective-permute-start(bf16[8,16,128]{2,1,0:T(8,128)(2,1)S(1)} %get-tuple-element.10), channel_id=1, source_target_pairs={{0,18},{2,16},{4,22},{6,20},{8,26},{10,24},{12,30},{14,28},{16,2},... | collective-permute-start | bytes 98312 | tf_op jit(solution)/shard_map/ppermute | solution.py:149
  6.8 0.0 collective-permute-done
  6.8 3.0 %collective-permute-done.2 = bf16[8,16,128]{2,1,0:T(8,128)(2,1)S(1)} collective-permute-done((bf16[8,16,128]{2,1,0:T(8,128)(2,1)S(1)}, bf16[8,16,128]{2,1,0:T(8,128)(2,1)S(1)}, u32[]{:S(2)}, u32[]{:S(2)}) %collective-permute-start.2) | collective-permute-done | bytes 32800 | tf_op jit(solution)/shard_map/ppermute | solution.py:154
  9.8 0.7 %collective-permute-done.1 = bf16[8,16,128]{2,1,0:T(8,128)(2,1)S(1)} collective-permute-done((bf16[8,16,128]{2,1,0:T(8,128)(2,1)S(1)}, bf16[8,16,128]{2,1,0:T(8,128)(2,1)S(1)}, u32[]{:S(2)}, u32[]{:S(2)}) %collective-permute-start.1) | collective-permute-done | bytes 32800 | tf_op jit(solution)/shard_map/ppermute | solution.py:149
  10.6 2.6 %collective-permute-start.3 = (bf16[2,8,16,128]{3,2,1,0:T(8,128)(2,1)S(1)}, bf16[2,8,16,128]{3,2,1,0:T(8,128)(2,1)S(1)}, u32[]{:S(2)}, u32[]{:S(2)}) collective-permute-start(bf16[2,8,16,128]{3,2,1,0:T(8,128)(2,1)S(1)} %pad_maximum_fusion), channel_id=1, source_target_pairs={{0,12},{2,14},{4,8},{6,10},{8,4},{10,6},{12,0},{14,2},{16,28},{18,... | collective-permute-start | bytes 196616 | tf_op jit(solution)/shard_map/ppermute | solution.py:157
  13.2 0.4 %collective-permute-start.4 = (bf16[2,8,16,128]{3,2,1,0:T(8,128)(2,1)S(1)}, bf16[2,8,16,128]{3,2,1,0:T(8,128)(2,1)S(1)}, u32[]{:S(2)}, u32[]{:S(2)}) collective-permute-start(bf16[2,8,16,128]{3,2,1,0:T(8,128)(2,1)S(1)} %pad_maximum_fusion), channel_id=1, source_target_pairs={{0,8},{2,10},{4,12},{6,14},{8,0},{10,2},{12,4},{14,6},{16,24},{18,... | collective-permute-start | bytes 196616 | tf_op jit(solution)/shard_map/ppermute | solution.py:157
  13.6 0.8 %collective-permute-start.5 = (bf16[2,8,16,128]{3,2,1,0:T(8,128)(2,1)S(1)}, bf16[2,8,16,128]{3,2,1,0:T(8,128)(2,1)S(1)}, u32[]{:S(2)}, u32[]{:S(2)}) collective-permute-start(bf16[2,8,16,128]{3,2,1,0:T(8,128)(2,1)S(1)} %pad_maximum_fusion), channel_id=1, source_target_pairs={{0,6},{2,4},{4,2},{6,0},{8,14},{10,12},{12,10},{14,8},{16,22},{18,... | collective-permute-start | bytes 196616 | tf_op jit(solution)/shard_map/ppermute | solution.py:157
  14.3 1.9 %collective-permute-done.3 = bf16[2,8,16,128]{3,2,1,0:T(8,128)(2,1)S(1)} collective-permute-done((bf16[2,8,16,128]{3,2,1,0:T(8,128)(2,1)S(1)}, bf16[2,8,16,128]{3,2,1,0:T(8,128)(2,1)S(1)}, u32[]{:S(2)}, u32[]{:S(2)}) %collective-permute-start.3) | collective-permute-done | bytes 65568 | tf_op jit(solution)/shard_map/ppermute | solution.py:157
  16.3 1.6 %collective-permute-done.4 = bf16[2,8,16,128]{3,2,1,0:T(8,128)(2,1)S(1)} collective-permute-done((bf16[2,8,16,128]{3,2,1,0:T(8,128)(2,1)S(1)}, bf16[2,8,16,128]{3,2,1,0:T(8,128)(2,1)S(1)}, u32[]{:S(2)}, u32[]{:S(2)}) %collective-permute-start.4) | collective-permute-done | bytes 65568 | tf_op jit(solution)/shard_map/ppermute | solution.py:157
  17.9 0.0 collective-permute-done.5
  18.0 0.2 collective-permute-start.6
  18.1 1.4 %collective-permute-done.6.got_ref = bf16[8,8,16,128]{3,2,1,0:T(8,128)(2,1)S(1)} collective-permute-done((bf16[8,8,16,128]{3,2,1,0:T(8,128)(2,1)S(1)}, bf16[8,8,16,128]{3,2,1,0:T(8,128)(2,1)S(1)}, u32[]{:S(2)}, u32[]{:S(2)}) %collective-permute-start.6) | collective-permute-done | bytes 262176 | tf_op jit(solution)/shard_map/ppermute | solution.py:159
  19.6 0.9 %shard_map.29 = f32[2,8,8,128]{3,2,1,0:T(8,128)} custom-call(bf16[8,8,16,128]{3,2,1,0:T(8,128)(2,1)S(1)} %constant_dynamic-update-slice_fusion.held_ref, bf16[8,8,16,128]{3,2,1,0:T(8,128)(2,1)S(1)} %collective-permute-done.6.got_ref), custom_call_target="tpu_custom_call" | custom-call | tf_op jit(solution)/shard_map/pallas_call | solution.py:126
  (6 shorter events, 0.1 us)
Async XLA Ops:
  1.6 5.2 %collective-permute-start = (bf16[8,16,128]{2,1,0:T(8,128)(2,1)S(1)}, bf16[8,16,128]{2,1,0:T(8,128)(2,1)S(1)}, u32[]{:S(2)}, u32[]{:S(2)}) collective-permute-start(bf16[8,16,128]{2,1,0:T(8,128)(2,1)S(1)} %bitcast.11), channel_id=1, source_target_pairs={{0,1},{1,0},{2,3},{3,2},{4,5},{5,4},{6,7},{7,6},{8,9},{9,8},{10,11... | collective-permute-start | bytes 98312 | tf_op jit(solution)/shard_map/ppermute | solution.py:153
  4.6 5.2 %collective-permute-start.2 = (bf16[8,16,128]{2,1,0:T(8,128)(2,1)S(1)}, bf16[8,16,128]{2,1,0:T(8,128)(2,1)S(1)}, u32[]{:S(2)}, u32[]{:S(2)}) collective-permute-start(bf16[8,16,128]{2,1,0:T(8,128)(2,1)S(1)} %bitcast.12), channel_id=1, source_target_pairs={{0,19},{1,18},{2,17},{3,16},{4,23},{5,22},{6,21},{7,20},{8,27},{9,... | collective-permute-start | bytes 98312 | tf_op jit(solution)/shard_map/ppermute | solution.py:154
  6.3 4.2 %collective-permute-start.1 = (bf16[8,16,128]{2,1,0:T(8,128)(2,1)S(1)}, bf16[8,16,128]{2,1,0:T(8,128)(2,1)S(1)}, u32[]{:S(2)}, u32[]{:S(2)}) collective-permute-start(bf16[8,16,128]{2,1,0:T(8,128)(2,1)S(1)} %get-tuple-element.10), channel_id=1, source_target_pairs={{0,18},{2,16},{4,22},{6,20},{8,26},{10,24},{12,30},{14,28},{16,2},... | collective-permute-start | bytes 98312 | tf_op jit(solution)/shard_map/ppermute | solution.py:149
  10.6 5.7 %collective-permute-start.3 = (bf16[2,8,16,128]{3,2,1,0:T(8,128)(2,1)S(1)}, bf16[2,8,16,128]{3,2,1,0:T(8,128)(2,1)S(1)}, u32[]{:S(2)}, u32[]{:S(2)}) collective-permute-start(bf16[2,8,16,128]{3,2,1,0:T(8,128)(2,1)S(1)} %pad_maximum_fusion), channel_id=1, source_target_pairs={{0,12},{2,14},{4,8},{6,10},{8,4},{10,6},{12,0},{14,2},{16,28},{18,... | collective-permute-start | bytes 196616 | tf_op jit(solution)/shard_map/ppermute | solution.py:157
  13.2 4.8 %collective-permute-start.4 = (bf16[2,8,16,128]{3,2,1,0:T(8,128)(2,1)S(1)}, bf16[2,8,16,128]{3,2,1,0:T(8,128)(2,1)S(1)}, u32[]{:S(2)}, u32[]{:S(2)}) collective-permute-start(bf16[2,8,16,128]{3,2,1,0:T(8,128)(2,1)S(1)} %pad_maximum_fusion), channel_id=1, source_target_pairs={{0,8},{2,10},{4,12},{6,14},{8,0},{10,2},{12,4},{14,6},{16,24},{18,... | collective-permute-start | bytes 196616 | tf_op jit(solution)/shard_map/ppermute | solution.py:157
  13.6 4.4 %collective-permute-start.5 = (bf16[2,8,16,128]{3,2,1,0:T(8,128)(2,1)S(1)}, bf16[2,8,16,128]{3,2,1,0:T(8,128)(2,1)S(1)}, u32[]{:S(2)}, u32[]{:S(2)}) collective-permute-start(bf16[2,8,16,128]{3,2,1,0:T(8,128)(2,1)S(1)} %pad_maximum_fusion), channel_id=1, source_target_pairs={{0,6},{2,4},{4,2},{6,0},{8,14},{10,12},{12,10},{14,8},{16,22},{18,... | collective-permute-start | bytes 196616 | tf_op jit(solution)/shard_map/ppermute | solution.py:157
  18.0 1.6 %collective-permute-start.6 = (bf16[8,8,16,128]{3,2,1,0:T(8,128)(2,1)S(1)}, bf16[8,8,16,128]{3,2,1,0:T(8,128)(2,1)S(1)}, u32[]{:S(2)}, u32[]{:S(2)}) collective-permute-start(bf16[8,8,16,128]{3,2,1,0:T(8,128)(2,1)S(1)} %constant_dynamic-update-slice_fusion.held_ref), channel_id=1, source_target_pairs={{0,2},{2,0},{4,6},{6,4},{8,10},{10,8},{12,14},{14,12},{16,18},{18,... | collective-permute-start | bytes 786440 | tf_op jit(solution)/shard_map/ppermute | solution.py:159

commit v4 on v3

--- a/solution.py
+++ b/solution.py
@@ -16,8 +16,9 @@
     planes, elems, chans, samples = v_ref.shape
     rows = w_ref.shape[0] // chans
     deep = elems * chans
-    loads = [pltpu.make_async_copy(w_ref, w16, sems.at[planes])]
-    loads += [pltpu.make_async_copy(v_ref.at[p], volts.at[p], sems.at[p]) for p in range(planes)]
+    loads = [
+        pltpu.make_async_copy(w_ref, w16, sems.at[0]), pltpu.make_async_copy(v_ref, volts, sems.at[1])
+    ]
     for load in loads:
         load.start()
     lane = lax.broadcasted_iota(jnp.int32, (elems, deep), 1)
@@ -33,11 +34,10 @@
     wide = wide.reshape(chans * rows, deep).astype(jnp.bfloat16)
     half = rows // 2
     loads[1].wait()
-    by_real = jnp.dot(wide, volts[0].reshape(deep, samples), preferred_element_type=jnp.float32)
-    by_real = by_real.reshape(chans, 2, half, samples)
-    loads[2].wait()
-    by_imag = jnp.dot(wide, volts[1].reshape(deep, samples), preferred_element_type=jnp.float32)
-    by_imag = by_imag.reshape(chans, 2, half, samples)
+    volts_both = jnp.concatenate([volts[p].reshape(deep, samples) for p in range(planes)], axis=1)
+    sums = jnp.dot(wide, volts_both, preferred_element_type=jnp.float32)
+    sums = sums.reshape(chans, 2, half, planes * samples)
+    by_real, by_imag = sums[..., :samples], sums[..., samples:]
     both[:, 0] = by_real[:, 0] + by_imag[:, 1]
     both[:, 1] = by_imag[:, 0] - by_real[:, 1]
     owned = chans // parts
@@ -68,7 +68,7 @@
             pltpu.VMEM((rows * chans, elems), jnp.float32),
             pltpu.VMEM((planes, elems, chans, samples), voltages.dtype),
             pltpu.VMEM((chans, planes, rows // planes, samples), jnp.float32),
-            pltpu.SemaphoreType.DMA((planes + 1,)),
+            pltpu.SemaphoreType.DMA((2,)),
         ],
     )(voltages[:, 0], weights.transpose(0, 1, 3, 2).reshape(rows * chans, elems))
 

time: 20.6 us -> 20.4 us (level)
  Pallas kernels: 2.46 us -> 2.23 us
    pallas_call x1, Pallas kernels: 1.55 us -> 1.33 us  [partial_beams(): pl.pallas_call(functools.partial(beam_kernel, parts), in_specs=[pl.BlockS...]
where the time goes in v4:
time: 20.4 us; the launch traced here: 20.3 us
  starting transfers between devices  9.13 us (45%)
  waiting for transfers between devices  8.77 us (43%)
  Pallas kernels  2.23 us (11%)
    ppermute x3, starting transfers between devices, body(): lax.ppermute(held, 'stn', [(i, i ^ step) for i in range(stations)])  3.78 us
    ppermute x3, waiting for transfers between devices, body(): lax.ppermute(held, 'stn', [(i, i ^ step) for i in range(stations)])  3.57 us
    ppermute x1, waiting for transfers between devices, body(): lax.ppermute(sent[step - 1], ('stn', 'elem'), there).astype(jnp.float32)  3.05 us
    ppermute x1, starting transfers between devices, body(): mine = mine + lax.ppermute(sent[step - 1], 'elem', here).astype(jnp.float32)  3.03 us
    ppermute x1, starting transfers between devices, body(): lax.ppermute(sent[step - 1], ('stn', 'elem'), there).astype(jnp.float32)  1.69 us
    ppermute x1, waiting for transfers between devices, body(): got = lax.ppermute(held, 'stn', [(i, i ^ 1) for i in range(stations)])  1.45 us
    pallas_call x1, Pallas kernels, partial_beams(): pl.pallas_call(functools.partial(beam_kernel, parts), in_specs=[pl.BlockS...  1.33 us
    pallas_call x1, Pallas kernels, cross_spectra(): pl.pallas_call(functools.partial(spectra_kernel, stages), out_shape=jax.S...  0.91 us
  transfers between devices with their start and end apart: 7, of which 5 were waited for; matrix products, arithmetic and copies ran while one was open for 0% of the time, Pallas kernels for 0%

profile of v4, /device:TPU:0, one launch (start us, length us, event | category | flops | bytes accessed | tf_op | source)
XLA Modules:
  0.0 20.3 jit_solution(15332892741400631408)
XLA Ops:
  0.0 1.3 %shard_map.28 = (f32[8,16,128]{2,1,0:T(8,128)S(1)}, bf16[8,16,128]{2,1,0:T(8,128)(2,1)S(1)}, bf16[1,8,16,128]{3,2,1,0:T(8,128)(2,1)S(1)}) custom-call(bf16[2,32,16,128]{3,2,1,0:T(8,128)(2,1)} %bitcast.13, bf16[256,32]{1,0:T(8,128)(2,1)} %bitcast.14), custom_call_target="tpu_custom_call" | custom-call | tf_op jit(solution)/shard_map/pallas_call | solution.py:56
  1.3 3.0 %collective-permute-start = (bf16[8,16,128]{2,1,0:T(8,128)(2,1)S(1)}, bf16[8,16,128]{2,1,0:T(8,128)(2,1)S(1)}, u32[]{:S(2)}, u32[]{:S(2)}) collective-permute-start(bf16[8,16,128]{2,1,0:T(8,128)(2,1)S(1)} %bitcast.11), channel_id=1, source_target_pairs={{0,1},{1,0},{2,3},{3,2},{4,5},{5,4},{6,7},{7,6},{8,9},{9,8},{10,11... | collective-permute-start | bytes 98312 | tf_op jit(solution)/shard_map/ppermute | solution.py:153
  4.4 1.7 %collective-permute-start.2 = (bf16[8,16,128]{2,1,0:T(8,128)(2,1)S(1)}, bf16[8,16,128]{2,1,0:T(8,128)(2,1)S(1)}, u32[]{:S(2)}, u32[]{:S(2)}) collective-permute-start(bf16[8,16,128]{2,1,0:T(8,128)(2,1)S(1)} %bitcast.12), channel_id=1, source_target_pairs={{0,19},{1,18},{2,17},{3,16},{4,23},{5,22},{6,21},{7,20},{8,27},{9,... | collective-permute-start | bytes 98312 | tf_op jit(solution)/shard_map/ppermute | solution.py:154
  6.1 0.5 %collective-permute-start.1 = (bf16[8,16,128]{2,1,0:T(8,128)(2,1)S(1)}, bf16[8,16,128]{2,1,0:T(8,128)(2,1)S(1)}, u32[]{:S(2)}, u32[]{:S(2)}) collective-permute-start(bf16[8,16,128]{2,1,0:T(8,128)(2,1)S(1)} %get-tuple-element.10), channel_id=1, source_target_pairs={{0,18},{2,16},{4,22},{6,20},{8,26},{10,24},{12,30},{14,28},{16,2},... | collective-permute-start | bytes 98312 | tf_op jit(solution)/shard_map/ppermute | solution.py:149
  6.5 0.0 collective-permute-done
  6.6 3.0 %collective-permute-done.2 = bf16[8,16,128]{2,1,0:T(8,128)(2,1)S(1)} collective-permute-done((bf16[8,16,128]{2,1,0:T(8,128)(2,1)S(1)}, bf16[8,16,128]{2,1,0:T(8,128)(2,1)S(1)}, u32[]{:S(2)}, u32[]{:S(2)}) %collective-permute-start.2) | collective-permute-done | bytes 32800 | tf_op jit(solution)/shard_map/ppermute | solution.py:154
  9.6 0.7 %collective-permute-done.1 = bf16[8,16,128]{2,1,0:T(8,128)(2,1)S(1)} collective-permute-done((bf16[8,16,128]{2,1,0:T(8,128)(2,1)S(1)}, bf16[8,16,128]{2,1,0:T(8,128)(2,1)S(1)}, u32[]{:S(2)}, u32[]{:S(2)}) %collective-permute-start.1) | collective-permute-done | bytes 32800 | tf_op jit(solution)/shard_map/ppermute | solution.py:149
  10.3 2.6 %collective-permute-start.3 = (bf16[2,8,16,128]{3,2,1,0:T(8,128)(2,1)S(1)}, bf16[2,8,16,128]{3,2,1,0:T(8,128)(2,1)S(1)}, u32[]{:S(2)}, u32[]{:S(2)}) collective-permute-start(bf16[2,8,16,128]{3,2,1,0:T(8,128)(2,1)S(1)} %pad_maximum_fusion), channel_id=1, source_target_pairs={{0,12},{2,14},{4,8},{6,10},{8,4},{10,6},{12,0},{14,2},{16,28},{18,... | collective-permute-start | bytes 196616 | tf_op jit(solution)/shard_map/ppermute | solution.py:157
  12.9 0.4 %collective-permute-start.4 = (bf16[2,8,16,128]{3,2,1,0:T(8,128)(2,1)S(1)}, bf16[2,8,16,128]{3,2,1,0:T(8,128)(2,1)S(1)}, u32[]{:S(2)}, u32[]{:S(2)}) collective-permute-start(bf16[2,8,16,128]{3,2,1,0:T(8,128)(2,1)S(1)} %pad_maximum_fusion), channel_id=1, source_target_pairs={{0,8},{2,10},{4,12},{6,14},{8,0},{10,2},{12,4},{14,6},{16,24},{18,... | collective-permute-start | bytes 196616 | tf_op jit(solution)/shard_map/ppermute | solution.py:157
  13.4 0.8 %collective-permute-start.5 = (bf16[2,8,16,128]{3,2,1,0:T(8,128)(2,1)S(1)}, bf16[2,8,16,128]{3,2,1,0:T(8,128)(2,1)S(1)}, u32[]{:S(2)}, u32[]{:S(2)}) collective-permute-start(bf16[2,8,16,128]{3,2,1,0:T(8,128)(2,1)S(1)} %pad_maximum_fusion), channel_id=1, source_target_pairs={{0,6},{2,4},{4,2},{6,0},{8,14},{10,12},{12,10},{14,8},{16,22},{18,... | collective-permute-start | bytes 196616 | tf_op jit(solution)/shard_map/ppermute | solution.py:157
  14.1 1.9 %collective-permute-done.3 = bf16[2,8,16,128]{3,2,1,0:T(8,128)(2,1)S(1)} collective-permute-done((bf16[2,8,16,128]{3,2,1,0:T(8,128)(2,1)S(1)}, bf16[2,8,16,128]{3,2,1,0:T(8,128)(2,1)S(1)}, u32[]{:S(2)}, u32[]{:S(2)}) %collective-permute-start.3) | collective-permute-done | bytes 65568 | tf_op jit(solution)/shard_map/ppermute | solution.py:157
  16.1 1.6 %collective-permute-done.4 = bf16[2,8,16,128]{3,2,1,0:T(8,128)(2,1)S(1)} collective-permute-done((bf16[2,8,16,128]{3,2,1,0:T(8,128)(2,1)S(1)}, bf16[2,8,16,128]{3,2,1,0:T(8,128)(2,1)S(1)}, u32[]{:S(2)}, u32[]{:S(2)}) %collective-permute-start.4) | collective-permute-done | bytes 65568 | tf_op jit(solution)/shard_map/ppermute | solution.py:157
  17.7 0.0 collective-permute-done.5
  17.7 0.2 collective-permute-start.6
  17.9 1.4 %collective-permute-done.6.got_ref = bf16[8,8,16,128]{3,2,1,0:T(8,128)(2,1)S(1)} collective-permute-done((bf16[8,8,16,128]{3,2,1,0:T(8,128)(2,1)S(1)}, bf16[8,8,16,128]{3,2,1,0:T(8,128)(2,1)S(1)}, u32[]{:S(2)}, u32[]{:S(2)}) %collective-permute-start.6) | collective-permute-done | bytes 262176 | tf_op jit(solution)/shard_map/ppermute | solution.py:159
  19.4 0.9 %shard_map.29 = f32[2,8,8,128]{3,2,1,0:T(8,128)} custom-call(bf16[8,8,16,128]{3,2,1,0:T(8,128)(2,1)S(1)} %constant_dynamic-update-slice_fusion.held_ref, bf16[8,8,16,128]{3,2,1,0:T(8,128)(2,1)S(1)} %collective-permute-done.6.got_ref), custom_call_target="tpu_custom_call" | custom-call | tf_op jit(solution)/shard_map/pallas_call | solution.py:126
  (6 shorter events, 0.1 us)
Async XLA Ops:
  1.3 5.2 %collective-permute-start = (bf16[8,16,128]{2,1,0:T(8,128)(2,1)S(1)}, bf16[8,16,128]{2,1,0:T(8,128)(2,1)S(1)}, u32[]{:S(2)}, u32[]{:S(2)}) collective-permute-start(bf16[8,16,128]{2,1,0:T(8,128)(2,1)S(1)} %bitcast.11), channel_id=1, source_target_pairs={{0,1},{1,0},{2,3},{3,2},{4,5},{5,4},{6,7},{7,6},{8,9},{9,8},{10,11... | collective-permute-start | bytes 98312 | tf_op jit(solution)/shard_map/ppermute | solution.py:153
  4.4 5.2 %collective-permute-start.2 = (bf16[8,16,128]{2,1,0:T(8,128)(2,1)S(1)}, bf16[8,16,128]{2,1,0:T(8,128)(2,1)S(1)}, u32[]{:S(2)}, u32[]{:S(2)}) collective-permute-start(bf16[8,16,128]{2,1,0:T(8,128)(2,1)S(1)} %bitcast.12), channel_id=1, source_target_pairs={{0,19},{1,18},{2,17},{3,16},{4,23},{5,22},{6,21},{7,20},{8,27},{9,... | collective-permute-start | bytes 98312 | tf_op jit(solution)/shard_map/ppermute | solution.py:154
  6.1 4.2 %collective-permute-start.1 = (bf16[8,16,128]{2,1,0:T(8,128)(2,1)S(1)}, bf16[8,16,128]{2,1,0:T(8,128)(2,1)S(1)}, u32[]{:S(2)}, u32[]{:S(2)}) collective-permute-start(bf16[8,16,128]{2,1,0:T(8,128)(2,1)S(1)} %get-tuple-element.10), channel_id=1, source_target_pairs={{0,18},{2,16},{4,22},{6,20},{8,26},{10,24},{12,30},{14,28},{16,2},... | collective-permute-start | bytes 98312 | tf_op jit(solution)/shard_map/ppermute | solution.py:149
  10.3 5.7 %collective-permute-start.3 = (bf16[2,8,16,128]{3,2,1,0:T(8,128)(2,1)S(1)}, bf16[2,8,16,128]{3,2,1,0:T(8,128)(2,1)S(1)}, u32[]{:S(2)}, u32[]{:S(2)}) collective-permute-start(bf16[2,8,16,128]{3,2,1,0:T(8,128)(2,1)S(1)} %pad_maximum_fusion), channel_id=1, source_target_pairs={{0,12},{2,14},{4,8},{6,10},{8,4},{10,6},{12,0},{14,2},{16,28},{18,... | collective-permute-start | bytes 196616 | tf_op jit(solution)/shard_map/ppermute | solution.py:157
  12.9 4.8 %collective-permute-start.4 = (bf16[2,8,16,128]{3,2,1,0:T(8,128)(2,1)S(1)}, bf16[2,8,16,128]{3,2,1,0:T(8,128)(2,1)S(1)}, u32[]{:S(2)}, u32[]{:S(2)}) collective-permute-start(bf16[2,8,16,128]{3,2,1,0:T(8,128)(2,1)S(1)} %pad_maximum_fusion), channel_id=1, source_target_pairs={{0,8},{2,10},{4,12},{6,14},{8,0},{10,2},{12,4},{14,6},{16,24},{18,... | collective-permute-start | bytes 196616 | tf_op jit(solution)/shard_map/ppermute | solution.py:157
  13.4 4.4 %collective-permute-start.5 = (bf16[2,8,16,128]{3,2,1,0:T(8,128)(2,1)S(1)}, bf16[2,8,16,128]{3,2,1,0:T(8,128)(2,1)S(1)}, u32[]{:S(2)}, u32[]{:S(2)}) collective-permute-start(bf16[2,8,16,128]{3,2,1,0:T(8,128)(2,1)S(1)} %pad_maximum_fusion), channel_id=1, source_target_pairs={{0,6},{2,4},{4,2},{6,0},{8,14},{10,12},{12,10},{14,8},{16,22},{18,... | collective-permute-start | bytes 196616 | tf_op jit(solution)/shard_map/ppermute | solution.py:157
  17.7 1.6 %collective-permute-start.6 = (bf16[8,8,16,128]{3,2,1,0:T(8,128)(2,1)S(1)}, bf16[8,8,16,128]{3,2,1,0:T(8,128)(2,1)S(1)}, u32[]{:S(2)}, u32[]{:S(2)}) collective-permute-start(bf16[8,8,16,128]{3,2,1,0:T(8,128)(2,1)S(1)} %constant_dynamic-update-slice_fusion.held_ref), channel_id=1, source_target_pairs={{0,2},{2,0},{4,6},{6,4},{8,10},{10,8},{12,14},{14,12},{16,18},{18,... | collective-permute-start | bytes 786440 | tf_op jit(solution)/shard_map/ppermute | solution.py:159

commit v5 on v4

--- a/solution.py
+++ b/solution.py
@@ -89,7 +89,7 @@
     return index, flip
 
 
-def spectra_kernel(stages, held_ref, got_ref, out_ref):
+def spectra_kernel(stages, held_ref, rows_ref, out_ref):
     chips, chans, rows, samples = held_ref.shape
     half = rows // 2
     me = lax.axis_index("stn")
@@ -101,33 +101,42 @@
     for c in range(chans):
         tiles = []
         for index, held_first in places:
-            held, got = held_ref[index, c], got_ref[index, c]
-            tiles += [jnp.where(held_first, held, got), jnp.where(held_first, got, held)]
+            held = held_ref[index, c]
+            tiles += [held, held]
         tiles = [t.astype(jnp.float32) for t in tiles]
         real = jnp.concatenate([t[:half] for t in tiles])
         imag = jnp.concatenate([t[half:] for t in tiles])
-        own = held_ref[0, c].astype(jnp.float32)
+        right = jnp.concatenate([real, imag], axis=1)
+        own = rows_ref[0, c].astype(jnp.float32)
         left = jnp.concatenate([own, jnp.concatenate([own[half:], -own[:half]])], axis=1)
-        right = jnp.concatenate([real, imag], axis=1)
         found.append(
             lax.dot_general(
                 left.astype(jnp.bfloat16), right.astype(jnp.bfloat16), (((1,), (1,)), ((), ())),
                 preferred_element_type=jnp.float32,
             )
         )
-    spec = jnp.concatenate(found).reshape(chans, 2, half, -1) / jnp.float32(samples)
+    spec = jnp.concatenate(found)
+    lane = lax.broadcasted_iota(jnp.int32, spec.shape, 1)
+    wanted = 0
+    for chip, (_, held_first) in enumerate(places):
+        first = jnp.where(held_first, 2 * chip * half, (2 * chip + 1) * half)
+        wanted = wanted + ((lane >= first) & (lane < first + half)).astype(jnp.int32)
+    spec = jnp.where(wanted > 0, spec, 0.0).reshape(chans, 2, half, -1) / jnp.float32(samples)
     out_ref[0] = spec[:, 0]
     out_ref[1] = spec[:, 1]
 
 
-def cross_spectra(held, got, stages):
+def half_spectra(held, block, stages):
     chips, chans, rows, samples = held.shape
     half = rows // 2
     return pl.pallas_call(
         functools.partial(spectra_kernel, stages),
         out_shape=jax.ShapeDtypeStruct((2, chans, half, 2 * chips * half), jnp.float32),
-        compiler_params=pltpu.CompilerParams(vmem_limit_bytes=room_for(held, got)),
-    )(held, got)
+        compiler_params=pltpu.CompilerParams(vmem_limit_bytes=room_for(held, block)),
+        cost_estimate=pl.CostEstimate(
+            flops=16 * held.size * half, bytes_accessed=2 * held.size, transcendentals=0
+        ),
+    )(held, block)
 
 
 def gather_plan(stations):
@@ -152,12 +161,15 @@
         there = [(s * parts + e, (s ^ near) * parts + f) for s in range(stations) for e, f in here]
         mine = mine + lax.ppermute(sent[step - 1], "elem", here).astype(jnp.float32)
         other = other + lax.ppermute(sent[step - 1], ("stn", "elem"), there).astype(jnp.float32)
-    held = jnp.stack([mine, other]).astype(jnp.bfloat16)
+    own = mine.astype(jnp.bfloat16)[None]
+    swap = [(i, i ^ 1) for i in range(stations)]
+    pair = lax.ppermute(own, "stn", swap)
+    held = jnp.concatenate([own, other.astype(jnp.bfloat16)[None]])
     for steps in stages:
         got = [lax.ppermute(held, "stn", [(i, i ^ step) for i in range(stations)]) for step in steps]
         held = jnp.concatenate([held] + got)
-    got = lax.ppermute(held, "stn", [(i, i ^ 1) for i in range(stations)])
-    return cross_spectra(held, got, [[near]] + stages)
+    theirs = half_spectra(held, pair, [[near]] + stages)
+    return half_spectra(held, own, [[near]] + stages) + lax.ppermute(theirs, "stn", swap)
 
 
 def solution(mesh):

time: 20.4 us -> 20.1 us (0.985)
  other arithmetic: 0.05 us -> 0.68 us
  waiting for transfers between devices: 8.77 us -> 8.26 us
  Pallas kernels: 2.23 us -> 1.81 us
    add x0 -> x1, other arithmetic: none -> 0.64 us  [body(): half_spectra(held, own, [[near]] + stages)]
    ppermute x1 -> x2, waiting for transfers between devices: 1.45 us -> 0.94 us  [the longest x1 0.94 us: body(): lax.ppermute(theirs, 'stn', swap)]
    pallas_call x1 -> x2, Pallas kernels: 0.91 us -> 0.48 us  [half_spectra(): pl.pallas_call(functools.partial(spectra_kernel, stages), out_shape=jax.S...]
  transfers between devices with their start and end apart: 7 -> 8, of which waited for: 5 -> 5; matrix products, arithmetic and copies ran while one was open for 0% -> 0% of each run, Pallas kernels for 0% -> 1%
where the time goes in v5:
time: 20.1 us; the launch traced here: 19.9 us
  starting transfers between devices  9.1 us (45%)
  waiting for transfers between devices  8.26 us (41%)
  Pallas kernels  1.81 us (9%)
  other arithmetic  0.68 us (3%)
    ppermute x3, starting transfers between devices, body(): lax.ppermute(held, 'stn', [(i, i ^ step) for i in range(stations)])  3.78 us
    ppermute x3, waiting for transfers between devices, body(): lax.ppermute(held, 'stn', [(i, i ^ step) for i in range(stations)])  3.57 us
    ppermute x1, waiting for transfers between devices, body(): lax.ppermute(sent[step - 1], ('stn', 'elem'), there).astype(jnp.float32)  3.05 us
    ppermute x1, starting transfers between devices, body(): mine = mine + lax.ppermute(sent[step - 1], 'elem', here).astype(jnp.float32)  3.03 us
    ppermute x1, starting transfers between devices, body(): lax.ppermute(sent[step - 1], ('stn', 'elem'), there).astype(jnp.float32)  1.69 us
    pallas_call x1, Pallas kernels, partial_beams(): pl.pallas_call(functools.partial(beam_kernel, parts), in_specs=[pl.BlockS...  1.33 us
    ppermute x1, waiting for transfers between devices, body(): lax.ppermute(theirs, 'stn', swap)  0.94 us
    ppermute x1, waiting for transfers between devices, body(): lax.ppermute(copy, 'stn', [(i, i ^ near) for i in range(stations)])  0.7 us
  transfers between devices with their start and end apart: 8, of which 5 were waited for; matrix products, arithmetic and copies ran while one was open for 0% of the time, Pallas kernels for 1%

profile of v5, /device:TPU:0, one launch (start us, length us, event | category | flops | bytes accessed | tf_op | source)
XLA Modules:
  0.0 19.9 jit_solution(13440406157295350703)
XLA Ops:
  0.0 1.3 %shard_map.28 = (f32[8,16,128]{2,1,0:T(8,128)S(1)}, bf16[8,16,128]{2,1,0:T(8,128)(2,1)S(1)}, bf16[1,8,16,128]{3,2,1,0:T(8,128)(2,1)S(1)}) custom-call(bf16[2,32,16,128]{3,2,1,0:T(8,128)(2,1)} %bitcast.13, bf16[256,32]{1,0:T(8,128)(2,1)} %bitcast.14), custom_call_target="tpu_custom_call" | custom-call | tf_op jit(solution)/shard_map/pallas_call | solution.py:56
  1.3 3.0 %collective-permute-start = (bf16[8,16,128]{2,1,0:T(8,128)(2,1)S(1)}, bf16[8,16,128]{2,1,0:T(8,128)(2,1)S(1)}, u32[]{:S(2)}, u32[]{:S(2)}) collective-permute-start(bf16[8,16,128]{2,1,0:T(8,128)(2,1)S(1)} %bitcast.11), channel_id=1, source_target_pairs={{0,1},{1,0},{2,3},{3,2},{4,5},{5,4},{6,7},{7,6},{8,9},{9,8},{10,11... | collective-permute-start | bytes 98312 | tf_op jit(solution)/shard_map/ppermute | solution.py:162
  4.4 1.7 %collective-permute-start.2 = (bf16[8,16,128]{2,1,0:T(8,128)(2,1)S(1)}, bf16[8,16,128]{2,1,0:T(8,128)(2,1)S(1)}, u32[]{:S(2)}, u32[]{:S(2)}) collective-permute-start(bf16[8,16,128]{2,1,0:T(8,128)(2,1)S(1)} %bitcast.12), channel_id=1, source_target_pairs={{0,19},{1,18},{2,17},{3,16},{4,23},{5,22},{6,21},{7,20},{8,27},{9,... | collective-permute-start | bytes 98312 | tf_op jit(solution)/shard_map/ppermute | solution.py:163
  6.1 0.5 %collective-permute-start.1 = (bf16[8,16,128]{2,1,0:T(8,128)(2,1)S(1)}, bf16[8,16,128]{2,1,0:T(8,128)(2,1)S(1)}, u32[]{:S(2)}, u32[]{:S(2)}) collective-permute-start(bf16[8,16,128]{2,1,0:T(8,128)(2,1)S(1)} %get-tuple-element.10), channel_id=1, source_target_pairs={{0,18},{2,16},{4,22},{6,20},{8,26},{10,24},{12,30},{14,28},{16,2},... | collective-permute-start | bytes 98312 | tf_op jit(solution)/shard_map/ppermute | solution.py:158
  6.5 0.0 collective-permute-done
  6.6 3.0 %collective-permute-done.2 = bf16[8,16,128]{2,1,0:T(8,128)(2,1)S(1)} collective-permute-done((bf16[8,16,128]{2,1,0:T(8,128)(2,1)S(1)}, bf16[8,16,128]{2,1,0:T(8,128)(2,1)S(1)}, u32[]{:S(2)}, u32[]{:S(2)}) %collective-permute-start.2) | collective-permute-done | bytes 32800 | tf_op jit(solution)/shard_map/ppermute | solution.py:163
  9.6 0.7 %collective-permute-done.1 = bf16[8,16,128]{2,1,0:T(8,128)(2,1)S(1)} collective-permute-done((bf16[8,16,128]{2,1,0:T(8,128)(2,1)S(1)}, bf16[8,16,128]{2,1,0:T(8,128)(2,1)S(1)}, u32[]{:S(2)}, u32[]{:S(2)}) %collective-permute-start.1) | collective-permute-done | bytes 32800 | tf_op jit(solution)/shard_map/ppermute | solution.py:158
  10.3 2.6 %collective-permute-start.3 = (bf16[2,8,16,128]{3,2,1,0:T(8,128)(2,1)S(1)}, bf16[2,8,16,128]{3,2,1,0:T(8,128)(2,1)S(1)}, u32[]{:S(2)}, u32[]{:S(2)}) collective-permute-start(bf16[2,8,16,128]{3,2,1,0:T(8,128)(2,1)S(1)} %pad_maximum_fusion), channel_id=1, source_target_pairs={{0,12},{2,14},{4,8},{6,10},{8,4},{10,6},{12,0},{14,2},{16,28},{18,... | collective-permute-start | bytes 196616 | tf_op jit(solution)/shard_map/ppermute | solution.py:169
  12.9 0.4 %collective-permute-start.4 = (bf16[2,8,16,128]{3,2,1,0:T(8,128)(2,1)S(1)}, bf16[2,8,16,128]{3,2,1,0:T(8,128)(2,1)S(1)}, u32[]{:S(2)}, u32[]{:S(2)}) collective-permute-start(bf16[2,8,16,128]{3,2,1,0:T(8,128)(2,1)S(1)} %pad_maximum_fusion), channel_id=1, source_target_pairs={{0,8},{2,10},{4,12},{6,14},{8,0},{10,2},{12,4},{14,6},{16,24},{18,... | collective-permute-start | bytes 196616 | tf_op jit(solution)/shard_map/ppermute | solution.py:169
  13.4 0.8 %collective-permute-start.5 = (bf16[2,8,16,128]{3,2,1,0:T(8,128)(2,1)S(1)}, bf16[2,8,16,128]{3,2,1,0:T(8,128)(2,1)S(1)}, u32[]{:S(2)}, u32[]{:S(2)}) collective-permute-start(bf16[2,8,16,128]{3,2,1,0:T(8,128)(2,1)S(1)} %pad_maximum_fusion), channel_id=1, source_target_pairs={{0,6},{2,4},{4,2},{6,0},{8,14},{10,12},{12,10},{14,8},{16,22},{18,... | collective-permute-start | bytes 196616 | tf_op jit(solution)/shard_map/ppermute | solution.py:169
  14.1 0.0 collective-permute-start.6
  14.1 1.9 %collective-permute-done.3 = bf16[2,8,16,128]{3,2,1,0:T(8,128)(2,1)S(1)} collective-permute-done((bf16[2,8,16,128]{3,2,1,0:T(8,128)(2,1)S(1)}, bf16[2,8,16,128]{3,2,1,0:T(8,128)(2,1)S(1)}, u32[]{:S(2)}, u32[]{:S(2)}) %collective-permute-start.3) | collective-permute-done | bytes 65568 | tf_op jit(solution)/shard_map/ppermute | solution.py:169
  16.1 1.6 %collective-permute-done.4 = bf16[2,8,16,128]{3,2,1,0:T(8,128)(2,1)S(1)} collective-permute-done((bf16[2,8,16,128]{3,2,1,0:T(8,128)(2,1)S(1)}, bf16[2,8,16,128]{3,2,1,0:T(8,128)(2,1)S(1)}, u32[]{:S(2)}, u32[]{:S(2)}) %collective-permute-start.4) | collective-permute-done | bytes 65568 | tf_op jit(solution)/shard_map/ppermute | solution.py:169
  17.7 0.0 collective-permute-done.5
  17.7 0.0 collective-permute-done.6.rows_ref
  17.8 0.3 %shard_map.30 = f32[2,8,8,128]{3,2,1,0:T(8,128)S(1)} custom-call(bf16[8,8,16,128]{3,2,1,0:T(8,128)(2,1)S(1)} %constant_dynamic-update-slice_fusion.held_ref, bf16[1,8,16,128]{3,2,1,0:T(8,128)(2,1)S(1)} %collective-permute-done.6.rows_ref), custom_call_target="tpu_custom_call" | custom-call | flops 16777216 | bytes 262144 | tf_op jit(solution)/shard_map/pallas_call | solution.py:132
  18.0 0.1 collective-permute-start.7
  18.1 0.2 %shard_map.29 = f32[2,8,8,128]{3,2,1,0:T(8,128)S(1)} custom-call(bf16[8,8,16,128]{3,2,1,0:T(8,128)(2,1)S(1)} %constant_dynamic-update-slice_fusion.held_ref, bf16[1,8,16,128]{3,2,1,0:T(8,128)(2,1)S(1)} %get-tuple-element.14.rows_ref), custom_call_target="tpu_custom_call" | custom-call | flops 16777216 | bytes 262144 | tf_op jit(solution)/shard_map/pallas_call | solution.py:132
  18.4 0.9 %collective-permute-done.7 = f32[2,8,8,128]{3,2,1,0:T(8,128)S(1)} collective-permute-done((f32[2,8,8,128]{3,2,1,0:T(8,128)S(1)}, f32[2,8,8,128]{3,2,1,0:T(8,128)S(1)}, u32[]{:S(2)}, u32[]{:S(2)}) %collective-permute-start.7) | collective-permute-done | bytes 65568 | tf_op jit(solution)/shard_map/ppermute | solution.py:172
  19.3 0.6 %add.11 = f32[2,8,8,128]{3,2,1,0:T(8,128)} add(f32[2,8,8,128]{3,2,1,0:T(8,128)S(1)} %shard_map.29, f32[2,8,8,128]{3,2,1,0:T(8,128)S(1)} %collective-permute-done.7) | non-fusion elementwise | flops 16384 | bytes 196608 | tf_op jit(solution)/shard_map/add | solution.py:172
  (6 shorter events, 0.1 us)
Async XLA Ops:
  1.3 5.2 %collective-permute-start = (bf16[8,16,128]{2,1,0:T(8,128)(2,1)S(1)}, bf16[8,16,128]{2,1,0:T(8,128)(2,1)S(1)}, u32[]{:S(2)}, u32[]{:S(2)}) collective-permute-start(bf16[8,16,128]{2,1,0:T(8,128)(2,1)S(1)} %bitcast.11), channel_id=1, source_target_pairs={{0,1},{1,0},{2,3},{3,2},{4,5},{5,4},{6,7},{7,6},{8,9},{9,8},{10,11... | collective-permute-start | bytes 98312 | tf_op jit(solution)/shard_map/ppermute | solution.py:162
  4.4 5.2 %collective-permute-start.2 = (bf16[8,16,128]{2,1,0:T(8,128)(2,1)S(1)}, bf16[8,16,128]{2,1,0:T(8,128)(2,1)S(1)}, u32[]{:S(2)}, u32[]{:S(2)}) collective-permute-start(bf16[8,16,128]{2,1,0:T(8,128)(2,1)S(1)} %bitcast.12), channel_id=1, source_target_pairs={{0,19},{1,18},{2,17},{3,16},{4,23},{5,22},{6,21},{7,20},{8,27},{9,... | collective-permute-start | bytes 98312 | tf_op jit(solution)/shard_map/ppermute | solution.py:163
  6.1 4.2 %collective-permute-start.1 = (bf16[8,16,128]{2,1,0:T(8,128)(2,1)S(1)}, bf16[8,16,128]{2,1,0:T(8,128)(2,1)S(1)}, u32[]{:S(2)}, u32[]{:S(2)}) collective-permute-start(bf16[8,16,128]{2,1,0:T(8,128)(2,1)S(1)} %get-tuple-element.10), channel_id=1, source_target_pairs={{0,18},{2,16},{4,22},{6,20},{8,26},{10,24},{12,30},{14,28},{16,2},... | collective-permute-start | bytes 98312 | tf_op jit(solution)/shard_map/ppermute | solution.py:158
  10.3 5.7 %collective-permute-start.3 = (bf16[2,8,16,128]{3,2,1,0:T(8,128)(2,1)S(1)}, bf16[2,8,16,128]{3,2,1,0:T(8,128)(2,1)S(1)}, u32[]{:S(2)}, u32[]{:S(2)}) collective-permute-start(bf16[2,8,16,128]{3,2,1,0:T(8,128)(2,1)S(1)} %pad_maximum_fusion), channel_id=1, source_target_pairs={{0,12},{2,14},{4,8},{6,10},{8,4},{10,6},{12,0},{14,2},{16,28},{18,... | collective-permute-start | bytes 196616 | tf_op jit(solution)/shard_map/ppermute | solution.py:169
  12.9 4.8 %collective-permute-start.4 = (bf16[2,8,16,128]{3,2,1,0:T(8,128)(2,1)S(1)}, bf16[2,8,16,128]{3,2,1,0:T(8,128)(2,1)S(1)}, u32[]{:S(2)}, u32[]{:S(2)}) collective-permute-start(bf16[2,8,16,128]{3,2,1,0:T(8,128)(2,1)S(1)} %pad_maximum_fusion), channel_id=1, source_target_pairs={{0,8},{2,10},{4,12},{6,14},{8,0},{10,2},{12,4},{14,6},{16,24},{18,... | collective-permute-start | bytes 196616 | tf_op jit(solution)/shard_map/ppermute | solution.py:169
  13.4 4.4 %collective-permute-start.5 = (bf16[2,8,16,128]{3,2,1,0:T(8,128)(2,1)S(1)}, bf16[2,8,16,128]{3,2,1,0:T(8,128)(2,1)S(1)}, u32[]{:S(2)}, u32[]{:S(2)}) collective-permute-start(bf16[2,8,16,128]{3,2,1,0:T(8,128)(2,1)S(1)} %pad_maximum_fusion), channel_id=1, source_target_pairs={{0,6},{2,4},{4,2},{6,0},{8,14},{10,12},{12,10},{14,8},{16,22},{18,... | collective-permute-start | bytes 196616 | tf_op jit(solution)/shard_map/ppermute | solution.py:169
  14.1 3.6 %collective-permute-start.6 = (bf16[1,8,16,128]{3,2,1,0:T(8,128)(2,1)S(1)}, bf16[1,8,16,128]{3,2,1,0:T(8,128)(2,1)S(1)}, u32[]{:S(2)}, u32[]{:S(2)}) collective-permute-start(bf16[1,8,16,128]{3,2,1,0:T(8,128)(2,1)S(1)} %get-tuple-element.14.rows_ref), channel_id=1, source_target_pairs={{0,2},{2,0},{4,6},{6,4},{8,10},{10,8},{12,14},{14,12},{16,18},{18,... | collective-permute-start | bytes 98312 | tf_op jit(solution)/shard_map/ppermute | solution.py:166
  18.0 1.3 %collective-permute-start.7 = (f32[2,8,8,128]{3,2,1,0:T(8,128)S(1)}, f32[2,8,8,128]{3,2,1,0:T(8,128)S(1)}, u32[]{:S(2)}, u32[]{:S(2)}) collective-permute-start(f32[2,8,8,128]{3,2,1,0:T(8,128)S(1)} %shard_map.30), channel_id=1, source_target_pairs={{0,2},{2,0},{4,6},{6,4},{8,10},{10,8},{12,14},{14,12},{16,18},{18,... | collective-permute-start | bytes 196616 | tf_op jit(solution)/shard_map/ppermute | solution.py:172

commit v6 on v5

--- a/solution.py
+++ b/solution.py
@@ -73,19 +73,21 @@
     )(voltages[:, 0], weights.transpose(0, 1, 3, 2).reshape(rows * chans, elems))
 
 
-def place_of(chip, stages):
+def place_of(chip, core, stages):
     index, flip, size = 0, 0, 1
-    for steps in stages:
-        bits = [s >> 1 for s in steps if (s >> 1) & ((s >> 1) - 1) == 0]
-        spots, flips = 0, 0
-        for at, step in enumerate(steps):
-            key = sum(1 << j for j, b in enumerate(bits) if (step >> 1) & b)
-            spots |= (at + 1) << (2 * key)
-            flips |= (step & 1) << key
+    for routes in stages:
+        bits = sorted({x for route in routes for x in route[:2] if x & (x - 1) == 0})
+        spots, flips = [0, 0], [0, 0]
+        for at, route in enumerate(routes):
+            for mine in range(2):
+                key = sum(1 << j for j, b in enumerate(bits) if route[mine ^ route[2]] & b)
+                spots[mine] |= (at + 1) << (2 * key)
+                flips[mine] |= route[2] << key
         key = sum(((chip >> (b.bit_length() - 1)) & 1) << j for j, b in enumerate(bits))
-        index = index + ((spots >> (2 * key)) & 3) * size
-        flip = flip ^ ((flips >> key) & 1)
-        size *= len(steps) + 1
+        spot = jnp.where(core == 0, spots[0], spots[1]) if spots[0] != spots[1] else spots[0]
+        index = index + ((spot >> (2 * key)) & 3) * size
+        flip = flip ^ ((flips[0] >> key) & 1)
+        size *= len(routes) + 1
     return index, flip
 
 
@@ -95,7 +97,7 @@
     me = lax.axis_index("stn")
     places = []
     for chip in range(chips):
-        index, flip = place_of((me >> 1) ^ chip, stages)
+        index, flip = place_of((me >> 1) ^ chip, me & 1, stages)
         places.append((index, ((me & 1) ^ flip) == 0))
     found = []
     for c in range(chans):
@@ -143,33 +145,43 @@
     bits = []
     while stations > 2:
         stations //= 2
-        bits.append(stations)
+        bits.append(stations // 2)
     first, rest = bits[0], bits[1:]
     stages = []
     while rest:
         pair, rest = rest[:2], rest[2:]
-        stages.append([sum(pair), pair[0], pair[1] + 1] if len(pair) == 2 else [pair[0] + 1])
-    return first + 1, stages
+        if len(pair) == 2:
+            low, high, both = pair[1], pair[0], sum(pair)
+            stages.append([(low, both, 0), (both, low, 0), (high, high, 1)])
+        else:
+            stages.append([(pair[0], pair[0], 1)])
+    return first, stages
+
+
+def across(block, route, stations):
+    pairs = [(i, i ^ (2 * route[i & 1] + route[2])) for i in range(stations)]
+    return lax.ppermute(block, "stn", pairs)
 
 
 def body(stations, parts, voltages, weights):
     mine, copy, sent = partial_beams(voltages, weights, parts)
     near, stages = gather_plan(stations)
-    other = lax.ppermute(copy, "stn", [(i, i ^ near) for i in range(stations)]).astype(jnp.float32)
+    first = (near, near, 1)
+    other = across(copy, first, stations).astype(jnp.float32)
     for step in range(1, parts):
         here = [(e, (e + step) % parts) for e in range(parts)]
-        there = [(s * parts + e, (s ^ near) * parts + f) for s in range(stations) for e, f in here]
+        there = [
+            (s * parts + e, (s ^ (2 * near + 1)) * parts + f) for s in range(stations) for e, f in here
+        ]
         mine = mine + lax.ppermute(sent[step - 1], "elem", here).astype(jnp.float32)
         other = other + lax.ppermute(sent[step - 1], ("stn", "elem"), there).astype(jnp.float32)
     own = mine.astype(jnp.bfloat16)[None]
-    swap = [(i, i ^ 1) for i in range(stations)]
-    pair = lax.ppermute(own, "stn", swap)
+    pair = across(own, (0, 0, 1), stations)
     held = jnp.concatenate([own, other.astype(jnp.bfloat16)[None]])
-    for steps in stages:
-        got = [lax.ppermute(held, "stn", [(i, i ^ step) for i in range(stations)]) for step in steps]
-        held = jnp.concatenate([held] + got)
-    theirs = half_spectra(held, pair, [[near]] + stages)
-    return half_spectra(held, own, [[near]] + stages) + lax.ppermute(theirs, "stn", swap)
+    for routes in stages:
+        held = jnp.concatenate([held] + [across(held, route, stations) for route in routes])
+    theirs = half_spectra(held, pair, [[first]] + stages)
+    return half_spectra(held, own, [[first]] + stages) + across(theirs, (0, 0, 1), stations)
 
 
 def solution(mesh):

time: 20.1 us -> 19.8 us (0.985)
  waiting for transfers between devices: 8.26 us -> 7.85 us
    ppermute x6, waiting for transfers between devices: 5.21 us -> 4.8 us  [across(): return lax.ppermute(block, 'stn', pairs)]
  transfers between devices with their start and end apart: 8 -> 8, of which waited for: 5 -> 6; matrix products, arithmetic and copies ran while one was open for 0% -> 0% of each run, Pallas kernels for 1% -> 1%
where the time goes in v6:
time: 19.8 us; the launch traced here: 19.7 us
  starting transfers between devices  9.26 us (47%)
  waiting for transfers between devices  7.85 us (40%)
  Pallas kernels  1.82 us (9%)
  other arithmetic  0.68 us (3%)
    ppermute x6, waiting for transfers between devices, across(): return lax.ppermute(block, 'stn', pairs)  4.8 us
    ppermute x6, starting transfers between devices, across(): return lax.ppermute(block, 'stn', pairs)  4.54 us
    ppermute x1, waiting for transfers between devices, body(): lax.ppermute(sent[step - 1], ('stn', 'elem'), there).astype(jnp.float32)  3.05 us
    ppermute x1, starting transfers between devices, body(): mine = mine + lax.ppermute(sent[step - 1], 'elem', here).astype(jnp.float32)  3.03 us
    ppermute x1, starting transfers between devices, body(): lax.ppermute(sent[step - 1], ('stn', 'elem'), there).astype(jnp.float32)  1.69 us
    pallas_call x1, Pallas kernels, partial_beams(): pl.pallas_call(functools.partial(beam_kernel, parts), in_specs=[pl.BlockS...  1.33 us
    add x1, other arithmetic, body(): half_spectra(held, own, [[first]] + stages)  0.64 us
    pallas_call x2, Pallas kernels, half_spectra(): pl.pallas_call(functools.partial(spectra_kernel, stages), out_shape=jax.S...  0.5 us
  transfers between devices with their start and end apart: 8, of which 6 were waited for; matrix products, arithmetic and copies ran while one was open for 0% of the time, Pallas kernels for 1%

profile of v6, /device:TPU:0, one launch (start us, length us, event | category | flops | bytes accessed | tf_op | source)
XLA Modules:
  0.0 19.7 jit_solution(5787279473155140454)
XLA Ops:
  0.0 1.3 %shard_map.28 = (f32[8,16,128]{2,1,0:T(8,128)S(1)}, bf16[8,16,128]{2,1,0:T(8,128)(2,1)S(1)}, bf16[1,8,16,128]{3,2,1,0:T(8,128)(2,1)S(1)}) custom-call(bf16[2,32,16,128]{3,2,1,0:T(8,128)(2,1)} %bitcast.13, bf16[256,32]{1,0:T(8,128)(2,1)} %bitcast.14), custom_call_target="tpu_custom_call" | custom-call | tf_op jit(solution)/shard_map/pallas_call | solution.py:56
  1.3 3.0 %collective-permute-start = (bf16[8,16,128]{2,1,0:T(8,128)(2,1)S(1)}, bf16[8,16,128]{2,1,0:T(8,128)(2,1)S(1)}, u32[]{:S(2)}, u32[]{:S(2)}) collective-permute-start(bf16[8,16,128]{2,1,0:T(8,128)(2,1)S(1)} %bitcast.11), channel_id=1, source_target_pairs={{0,1},{1,0},{2,3},{3,2},{4,5},{5,4},{6,7},{7,6},{8,9},{9,8},{10,11... | collective-permute-start | bytes 98312 | tf_op jit(solution)/shard_map/ppermute | solution.py:176
  4.4 1.7 %collective-permute-start.2 = (bf16[8,16,128]{2,1,0:T(8,128)(2,1)S(1)}, bf16[8,16,128]{2,1,0:T(8,128)(2,1)S(1)}, u32[]{:S(2)}, u32[]{:S(2)}) collective-permute-start(bf16[8,16,128]{2,1,0:T(8,128)(2,1)S(1)} %bitcast.12), channel_id=1, source_target_pairs={{0,19},{1,18},{2,17},{3,16},{4,23},{5,22},{6,21},{7,20},{8,27},{9,... | collective-permute-start | bytes 98312 | tf_op jit(solution)/shard_map/ppermute | solution.py:177
  6.1 0.5 %collective-permute-start.1 = (bf16[8,16,128]{2,1,0:T(8,128)(2,1)S(1)}, bf16[8,16,128]{2,1,0:T(8,128)(2,1)S(1)}, u32[]{:S(2)}, u32[]{:S(2)}) collective-permute-start(bf16[8,16,128]{2,1,0:T(8,128)(2,1)S(1)} %get-tuple-element.10), channel_id=1, source_target_pairs={{0,18},{2,16},{4,22},{6,20},{8,26},{10,24},{12,30},{14,28},{16,2},... | collective-permute-start | bytes 98312 | tf_op jit(solution)/shard_map/ppermute | solution.py:163
  6.5 0.0 collective-permute-done
  6.6 3.0 %collective-permute-done.2 = bf16[8,16,128]{2,1,0:T(8,128)(2,1)S(1)} collective-permute-done((bf16[8,16,128]{2,1,0:T(8,128)(2,1)S(1)}, bf16[8,16,128]{2,1,0:T(8,128)(2,1)S(1)}, u32[]{:S(2)}, u32[]{:S(2)}) %collective-permute-start.2) | collective-permute-done | bytes 32800 | tf_op jit(solution)/shard_map/ppermute | solution.py:177
  9.6 0.7 %collective-permute-done.1 = bf16[8,16,128]{2,1,0:T(8,128)(2,1)S(1)} collective-permute-done((bf16[8,16,128]{2,1,0:T(8,128)(2,1)S(1)}, bf16[8,16,128]{2,1,0:T(8,128)(2,1)S(1)}, u32[]{:S(2)}, u32[]{:S(2)}) %collective-permute-start.1) | collective-permute-done | bytes 32800 | tf_op jit(solution)/shard_map/ppermute | solution.py:163
  10.3 1.6 %collective-permute-start.3 = (bf16[2,8,16,128]{3,2,1,0:T(8,128)(2,1)S(1)}, bf16[2,8,16,128]{3,2,1,0:T(8,128)(2,1)S(1)}, u32[]{:S(2)}, u32[]{:S(2)}) collective-permute-start(bf16[2,8,16,128]{3,2,1,0:T(8,128)(2,1)S(1)} %pad_maximum_fusion), channel_id=1, source_target_pairs={{0,4},{2,14},{4,0},{6,10},{8,12},{10,6},{12,8},{14,2},{16,20},{18,... | collective-permute-start | bytes 196616 | tf_op jit(solution)/shard_map/ppermute | solution.py:163
  11.9 1.6 %collective-permute-start.4 = (bf16[2,8,16,128]{3,2,1,0:T(8,128)(2,1)S(1)}, bf16[2,8,16,128]{3,2,1,0:T(8,128)(2,1)S(1)}, u32[]{:S(2)}, u32[]{:S(2)}) collective-permute-start(bf16[2,8,16,128]{3,2,1,0:T(8,128)(2,1)S(1)} %pad_maximum_fusion), channel_id=1, source_target_pairs={{0,12},{2,6},{4,8},{6,2},{8,4},{10,14},{12,0},{14,10},{16,28},{18,... | collective-permute-start | bytes 196616 | tf_op jit(solution)/shard_map/ppermute | solution.py:163
  13.5 0.7 %collective-permute-start.5 = (bf16[2,8,16,128]{3,2,1,0:T(8,128)(2,1)S(1)}, bf16[2,8,16,128]{3,2,1,0:T(8,128)(2,1)S(1)}, u32[]{:S(2)}, u32[]{:S(2)}) collective-permute-start(bf16[2,8,16,128]{3,2,1,0:T(8,128)(2,1)S(1)} %pad_maximum_fusion), channel_id=1, source_target_pairs={{0,10},{2,8},{4,14},{6,12},{8,2},{10,0},{12,6},{14,4},{16,26},{18,... | collective-permute-start | bytes 196616 | tf_op jit(solution)/shard_map/ppermute | solution.py:163
  14.1 0.0 collective-permute-start.6
  14.1 0.5 %collective-permute-done.3 = bf16[2,8,16,128]{3,2,1,0:T(8,128)(2,1)S(1)} collective-permute-done((bf16[2,8,16,128]{3,2,1,0:T(8,128)(2,1)S(1)}, bf16[2,8,16,128]{3,2,1,0:T(8,128)(2,1)S(1)}, u32[]{:S(2)}, u32[]{:S(2)}) %collective-permute-start.3) | collective-permute-done | bytes 65568 | tf_op jit(solution)/shard_map/ppermute | solution.py:163
  14.7 2.5 %collective-permute-done.4 = bf16[2,8,16,128]{3,2,1,0:T(8,128)(2,1)S(1)} collective-permute-done((bf16[2,8,16,128]{3,2,1,0:T(8,128)(2,1)S(1)}, bf16[2,8,16,128]{3,2,1,0:T(8,128)(2,1)S(1)}, u32[]{:S(2)}, u32[]{:S(2)}) %collective-permute-start.4) | collective-permute-done | bytes 65568 | tf_op jit(solution)/shard_map/ppermute | solution.py:163
  17.2 0.3 %collective-permute-done.5 = bf16[2,8,16,128]{3,2,1,0:T(8,128)(2,1)S(1)} collective-permute-done((bf16[2,8,16,128]{3,2,1,0:T(8,128)(2,1)S(1)}, bf16[2,8,16,128]{3,2,1,0:T(8,128)(2,1)S(1)}, u32[]{:S(2)}, u32[]{:S(2)}) %collective-permute-start.5) | collective-permute-done | bytes 65568 | tf_op jit(solution)/shard_map/ppermute | solution.py:163
  17.5 0.0 collective-permute-done.6.rows_ref
  17.5 0.3 %shard_map.30 = f32[2,8,8,128]{3,2,1,0:T(8,128)S(1)} custom-call(bf16[8,8,16,128]{3,2,1,0:T(8,128)(2,1)S(1)} %constant_dynamic-update-slice_fusion.held_ref, bf16[1,8,16,128]{3,2,1,0:T(8,128)(2,1)S(1)} %collective-permute-done.6.rows_ref), custom_call_target="tpu_custom_call" | custom-call | flops 16777216 | bytes 262144 | tf_op jit(solution)/shard_map/pallas_call | solution.py:134
  17.8 0.3 %collective-permute-start.7 = (f32[2,8,8,128]{3,2,1,0:T(8,128)S(1)}, f32[2,8,8,128]{3,2,1,0:T(8,128)S(1)}, u32[]{:S(2)}, u32[]{:S(2)}) collective-permute-start(f32[2,8,8,128]{3,2,1,0:T(8,128)S(1)} %shard_map.30), channel_id=1, source_target_pairs={{0,2},{2,0},{4,6},{6,4},{8,10},{10,8},{12,14},{14,12},{16,18},{18,... | collective-permute-start | bytes 196616 | tf_op jit(solution)/shard_map/ppermute | solution.py:163
  18.1 0.2 %shard_map.29 = f32[2,8,8,128]{3,2,1,0:T(8,128)S(1)} custom-call(bf16[8,8,16,128]{3,2,1,0:T(8,128)(2,1)S(1)} %constant_dynamic-update-slice_fusion.held_ref, bf16[1,8,16,128]{3,2,1,0:T(8,128)(2,1)S(1)} %get-tuple-element.14.rows_ref), custom_call_target="tpu_custom_call" | custom-call | flops 16777216 | bytes 262144 | tf_op jit(solution)/shard_map/pallas_call | solution.py:134
  18.3 0.8 %collective-permute-done.7 = f32[2,8,8,128]{3,2,1,0:T(8,128)S(1)} collective-permute-done((f32[2,8,8,128]{3,2,1,0:T(8,128)S(1)}, f32[2,8,8,128]{3,2,1,0:T(8,128)S(1)}, u32[]{:S(2)}, u32[]{:S(2)}) %collective-permute-start.7) | collective-permute-done | bytes 65568 | tf_op jit(solution)/shard_map/ppermute | solution.py:163
  19.1 0.6 %add.11 = f32[2,8,8,128]{3,2,1,0:T(8,128)} add(f32[2,8,8,128]{3,2,1,0:T(8,128)S(1)} %shard_map.29, f32[2,8,8,128]{3,2,1,0:T(8,128)S(1)} %collective-permute-done.7) | non-fusion elementwise | flops 16384 | bytes 196608 | tf_op jit(solution)/shard_map/add | solution.py:184
  (6 shorter events, 0.1 us)
Async XLA Ops:
  1.3 5.2 %collective-permute-start = (bf16[8,16,128]{2,1,0:T(8,128)(2,1)S(1)}, bf16[8,16,128]{2,1,0:T(8,128)(2,1)S(1)}, u32[]{:S(2)}, u32[]{:S(2)}) collective-permute-start(bf16[8,16,128]{2,1,0:T(8,128)(2,1)S(1)} %bitcast.11), channel_id=1, source_target_pairs={{0,1},{1,0},{2,3},{3,2},{4,5},{5,4},{6,7},{7,6},{8,9},{9,8},{10,11... | collective-permute-start | bytes 98312 | tf_op jit(solution)/shard_map/ppermute | solution.py:176
  4.4 5.2 %collective-permute-start.2 = (bf16[8,16,128]{2,1,0:T(8,128)(2,1)S(1)}, bf16[8,16,128]{2,1,0:T(8,128)(2,1)S(1)}, u32[]{:S(2)}, u32[]{:S(2)}) collective-permute-start(bf16[8,16,128]{2,1,0:T(8,128)(2,1)S(1)} %bitcast.12), channel_id=1, source_target_pairs={{0,19},{1,18},{2,17},{3,16},{4,23},{5,22},{6,21},{7,20},{8,27},{9,... | collective-permute-start | bytes 98312 | tf_op jit(solution)/shard_map/ppermute | solution.py:177
  6.1 4.2 %collective-permute-start.1 = (bf16[8,16,128]{2,1,0:T(8,128)(2,1)S(1)}, bf16[8,16,128]{2,1,0:T(8,128)(2,1)S(1)}, u32[]{:S(2)}, u32[]{:S(2)}) collective-permute-start(bf16[8,16,128]{2,1,0:T(8,128)(2,1)S(1)} %get-tuple-element.10), channel_id=1, source_target_pairs={{0,18},{2,16},{4,22},{6,20},{8,26},{10,24},{12,30},{14,28},{16,2},... | collective-permute-start | bytes 98312 | tf_op jit(solution)/shard_map/ppermute | solution.py:163
  10.3 4.3 %collective-permute-start.3 = (bf16[2,8,16,128]{3,2,1,0:T(8,128)(2,1)S(1)}, bf16[2,8,16,128]{3,2,1,0:T(8,128)(2,1)S(1)}, u32[]{:S(2)}, u32[]{:S(2)}) collective-permute-start(bf16[2,8,16,128]{3,2,1,0:T(8,128)(2,1)S(1)} %pad_maximum_fusion), channel_id=1, source_target_pairs={{0,4},{2,14},{4,0},{6,10},{8,12},{10,6},{12,8},{14,2},{16,20},{18,... | collective-permute-start | bytes 196616 | tf_op jit(solution)/shard_map/ppermute | solution.py:163
  11.9 5.3 %collective-permute-start.4 = (bf16[2,8,16,128]{3,2,1,0:T(8,128)(2,1)S(1)}, bf16[2,8,16,128]{3,2,1,0:T(8,128)(2,1)S(1)}, u32[]{:S(2)}, u32[]{:S(2)}) collective-permute-start(bf16[2,8,16,128]{3,2,1,0:T(8,128)(2,1)S(1)} %pad_maximum_fusion), channel_id=1, source_target_pairs={{0,12},{2,6},{4,8},{6,2},{8,4},{10,14},{12,0},{14,10},{16,28},{18,... | collective-permute-start | bytes 196616 | tf_op jit(solution)/shard_map/ppermute | solution.py:163
  13.5 4.0 %collective-permute-start.5 = (bf16[2,8,16,128]{3,2,1,0:T(8,128)(2,1)S(1)}, bf16[2,8,16,128]{3,2,1,0:T(8,128)(2,1)S(1)}, u32[]{:S(2)}, u32[]{:S(2)}) collective-permute-start(bf16[2,8,16,128]{3,2,1,0:T(8,128)(2,1)S(1)} %pad_maximum_fusion), channel_id=1, source_target_pairs={{0,10},{2,8},{4,14},{6,12},{8,2},{10,0},{12,6},{14,4},{16,26},{18,... | collective-permute-start | bytes 196616 | tf_op jit(solution)/shard_map/ppermute | solution.py:163
  14.1 3.4 %collective-permute-start.6 = (bf16[1,8,16,128]{3,2,1,0:T(8,128)(2,1)S(1)}, bf16[1,8,16,128]{3,2,1,0:T(8,128)(2,1)S(1)}, u32[]{:S(2)}, u32[]{:S(2)}) collective-permute-start(bf16[1,8,16,128]{3,2,1,0:T(8,128)(2,1)S(1)} %get-tuple-element.14.rows_ref), channel_id=1, source_target_pairs={{0,2},{2,0},{4,6},{6,4},{8,10},{10,8},{12,14},{14,12},{16,18},{18,... | collective-permute-start | bytes 98312 | tf_op jit(solution)/shard_map/ppermute | solution.py:163
  17.8 1.3 %collective-permute-start.7 = (f32[2,8,8,128]{3,2,1,0:T(8,128)S(1)}, f32[2,8,8,128]{3,2,1,0:T(8,128)S(1)}, u32[]{:S(2)}, u32[]{:S(2)}) collective-permute-start(f32[2,8,8,128]{3,2,1,0:T(8,128)S(1)} %shard_map.30), channel_id=1, source_target_pairs={{0,2},{2,0},{4,6},{6,4},{8,10},{10,8},{12,14},{14,12},{16,18},{18,... | collective-permute-start | bytes 196616 | tf_op jit(solution)/shard_map/ppermute | solution.py:163

commit v7 on v6

--- a/solution.py
+++ b/solution.py
@@ -118,12 +118,12 @@
             )
         )
     spec = jnp.concatenate(found)
-    lane = lax.broadcasted_iota(jnp.int32, spec.shape, 1)
-    wanted = 0
+    lane = lax.broadcasted_iota(jnp.int32, (1, spec.shape[1]), 1)
+    scale = jnp.zeros(lane.shape, jnp.float32)
     for chip, (_, held_first) in enumerate(places):
         first = jnp.where(held_first, 2 * chip * half, (2 * chip + 1) * half)
-        wanted = wanted + ((lane >= first) & (lane < first + half)).astype(jnp.int32)
-    spec = jnp.where(wanted > 0, spec, 0.0).reshape(chans, 2, half, -1) / jnp.float32(samples)
+        scale = jnp.where((lane >= first) & (lane < first + half), 1.0, scale)
+    spec = (spec * scale).reshape(chans, 2, half, -1) / jnp.float32(samples)
     out_ref[0] = spec[:, 0]
     out_ref[1] = spec[:, 1]
 

time: 19.8 us -> 19.8 us (level)
  no operation moved by 1% of the time
where the time goes in v7:
time: 19.8 us; the launch traced here: 19.7 us
  starting transfers between devices  9.26 us (47%)
  waiting for transfers between devices  7.85 us (40%)
  Pallas kernels  1.82 us (9%)
  other arithmetic  0.68 us (3%)
    ppermute x6, waiting for transfers between devices, across(): return lax.ppermute(block, 'stn', pairs)  4.8 us
    ppermute x6, starting transfers between devices, across(): return lax.ppermute(block, 'stn', pairs)  4.54 us
    ppermute x1, waiting for transfers between devices, body(): lax.ppermute(sent[step - 1], ('stn', 'elem'), there).astype(jnp.float32)  3.05 us
    ppermute x1, starting transfers between devices, body(): mine = mine + lax.ppermute(sent[step - 1], 'elem', here).astype(jnp.float32)  3.03 us
    ppermute x1, starting transfers between devices, body(): lax.ppermute(sent[step - 1], ('stn', 'elem'), there).astype(jnp.float32)  1.69 us
    pallas_call x1, Pallas kernels, partial_beams(): pl.pallas_call(functools.partial(beam_kernel, parts), in_specs=[pl.BlockS...  1.33 us
    add x1, other arithmetic, body(): half_spectra(held, own, [[first]] + stages)  0.64 us
    pallas_call x2, Pallas kernels, half_spectra(): pl.pallas_call(functools.partial(spectra_kernel, stages), out_shape=jax.S...  0.49 us
  transfers between devices with their start and end apart: 8, of which 6 were waited for; matrix products, arithmetic and copies ran while one was open for 0% of the time, Pallas kernels for 1%

profile of v7, /device:TPU:0, one launch (start us, length us, event | category | flops | bytes accessed | tf_op | source)
XLA Modules:
  0.0 19.7 jit_solution(12881369724777171245)
XLA Ops:
  0.0 1.3 %shard_map.28 = (f32[8,16,128]{2,1,0:T(8,128)S(1)}, bf16[8,16,128]{2,1,0:T(8,128)(2,1)S(1)}, bf16[1,8,16,128]{3,2,1,0:T(8,128)(2,1)S(1)}) custom-call(bf16[2,32,16,128]{3,2,1,0:T(8,128)(2,1)} %bitcast.13, bf16[256,32]{1,0:T(8,128)(2,1)} %bitcast.14), custom_call_target="tpu_custom_call" | custom-call | tf_op jit(solution)/shard_map/pallas_call | solution.py:56
  1.3 3.0 %collective-permute-start = (bf16[8,16,128]{2,1,0:T(8,128)(2,1)S(1)}, bf16[8,16,128]{2,1,0:T(8,128)(2,1)S(1)}, u32[]{:S(2)}, u32[]{:S(2)}) collective-permute-start(bf16[8,16,128]{2,1,0:T(8,128)(2,1)S(1)} %bitcast.11), channel_id=1, source_target_pairs={{0,1},{1,0},{2,3},{3,2},{4,5},{5,4},{6,7},{7,6},{8,9},{9,8},{10,11... | collective-permute-start | bytes 98312 | tf_op jit(solution)/shard_map/ppermute | solution.py:176
  4.4 1.7 %collective-permute-start.2 = (bf16[8,16,128]{2,1,0:T(8,128)(2,1)S(1)}, bf16[8,16,128]{2,1,0:T(8,128)(2,1)S(1)}, u32[]{:S(2)}, u32[]{:S(2)}) collective-permute-start(bf16[8,16,128]{2,1,0:T(8,128)(2,1)S(1)} %bitcast.12), channel_id=1, source_target_pairs={{0,19},{1,18},{2,17},{3,16},{4,23},{5,22},{6,21},{7,20},{8,27},{9,... | collective-permute-start | bytes 98312 | tf_op jit(solution)/shard_map/ppermute | solution.py:177
  6.1 0.5 %collective-permute-start.1 = (bf16[8,16,128]{2,1,0:T(8,128)(2,1)S(1)}, bf16[8,16,128]{2,1,0:T(8,128)(2,1)S(1)}, u32[]{:S(2)}, u32[]{:S(2)}) collective-permute-start(bf16[8,16,128]{2,1,0:T(8,128)(2,1)S(1)} %get-tuple-element.10), channel_id=1, source_target_pairs={{0,18},{2,16},{4,22},{6,20},{8,26},{10,24},{12,30},{14,28},{16,2},... | collective-permute-start | bytes 98312 | tf_op jit(solution)/shard_map/ppermute | solution.py:163
  6.5 0.0 collective-permute-done
  6.6 3.0 %collective-permute-done.2 = bf16[8,16,128]{2,1,0:T(8,128)(2,1)S(1)} collective-permute-done((bf16[8,16,128]{2,1,0:T(8,128)(2,1)S(1)}, bf16[8,16,128]{2,1,0:T(8,128)(2,1)S(1)}, u32[]{:S(2)}, u32[]{:S(2)}) %collective-permute-start.2) | collective-permute-done | bytes 32800 | tf_op jit(solution)/shard_map/ppermute | solution.py:177
  9.6 0.7 %collective-permute-done.1 = bf16[8,16,128]{2,1,0:T(8,128)(2,1)S(1)} collective-permute-done((bf16[8,16,128]{2,1,0:T(8,128)(2,1)S(1)}, bf16[8,16,128]{2,1,0:T(8,128)(2,1)S(1)}, u32[]{:S(2)}, u32[]{:S(2)}) %collective-permute-start.1) | collective-permute-done | bytes 32800 | tf_op jit(solution)/shard_map/ppermute | solution.py:163
  10.3 1.6 %collective-permute-start.3 = (bf16[2,8,16,128]{3,2,1,0:T(8,128)(2,1)S(1)}, bf16[2,8,16,128]{3,2,1,0:T(8,128)(2,1)S(1)}, u32[]{:S(2)}, u32[]{:S(2)}) collective-permute-start(bf16[2,8,16,128]{3,2,1,0:T(8,128)(2,1)S(1)} %pad_maximum_fusion), channel_id=1, source_target_pairs={{0,4},{2,14},{4,0},{6,10},{8,12},{10,6},{12,8},{14,2},{16,20},{18,... | collective-permute-start | bytes 196616 | tf_op jit(solution)/shard_map/ppermute | solution.py:163
  11.9 1.6 %collective-permute-start.4 = (bf16[2,8,16,128]{3,2,1,0:T(8,128)(2,1)S(1)}, bf16[2,8,16,128]{3,2,1,0:T(8,128)(2,1)S(1)}, u32[]{:S(2)}, u32[]{:S(2)}) collective-permute-start(bf16[2,8,16,128]{3,2,1,0:T(8,128)(2,1)S(1)} %pad_maximum_fusion), channel_id=1, source_target_pairs={{0,12},{2,6},{4,8},{6,2},{8,4},{10,14},{12,0},{14,10},{16,28},{18,... | collective-permute-start | bytes 196616 | tf_op jit(solution)/shard_map/ppermute | solution.py:163
  13.5 0.7 %collective-permute-start.5 = (bf16[2,8,16,128]{3,2,1,0:T(8,128)(2,1)S(1)}, bf16[2,8,16,128]{3,2,1,0:T(8,128)(2,1)S(1)}, u32[]{:S(2)}, u32[]{:S(2)}) collective-permute-start(bf16[2,8,16,128]{3,2,1,0:T(8,128)(2,1)S(1)} %pad_maximum_fusion), channel_id=1, source_target_pairs={{0,10},{2,8},{4,14},{6,12},{8,2},{10,0},{12,6},{14,4},{16,26},{18,... | collective-permute-start | bytes 196616 | tf_op jit(solution)/shard_map/ppermute | solution.py:163
  14.1 0.0 collective-permute-start.6
  14.1 0.5 %collective-permute-done.3 = bf16[2,8,16,128]{3,2,1,0:T(8,128)(2,1)S(1)} collective-permute-done((bf16[2,8,16,128]{3,2,1,0:T(8,128)(2,1)S(1)}, bf16[2,8,16,128]{3,2,1,0:T(8,128)(2,1)S(1)}, u32[]{:S(2)}, u32[]{:S(2)}) %collective-permute-start.3) | collective-permute-done | bytes 65568 | tf_op jit(solution)/shard_map/ppermute | solution.py:163
  14.7 2.5 %collective-permute-done.4 = bf16[2,8,16,128]{3,2,1,0:T(8,128)(2,1)S(1)} collective-permute-done((bf16[2,8,16,128]{3,2,1,0:T(8,128)(2,1)S(1)}, bf16[2,8,16,128]{3,2,1,0:T(8,128)(2,1)S(1)}, u32[]{:S(2)}, u32[]{:S(2)}) %collective-permute-start.4) | collective-permute-done | bytes 65568 | tf_op jit(solution)/shard_map/ppermute | solution.py:163
  17.2 0.3 %collective-permute-done.5 = bf16[2,8,16,128]{3,2,1,0:T(8,128)(2,1)S(1)} collective-permute-done((bf16[2,8,16,128]{3,2,1,0:T(8,128)(2,1)S(1)}, bf16[2,8,16,128]{3,2,1,0:T(8,128)(2,1)S(1)}, u32[]{:S(2)}, u32[]{:S(2)}) %collective-permute-start.5) | collective-permute-done | bytes 65568 | tf_op jit(solution)/shard_map/ppermute | solution.py:163
  17.5 0.0 collective-permute-done.6.rows_ref
  17.5 0.3 %shard_map.30 = f32[2,8,8,128]{3,2,1,0:T(8,128)S(1)} custom-call(bf16[8,8,16,128]{3,2,1,0:T(8,128)(2,1)S(1)} %constant_dynamic-update-slice_fusion.held_ref, bf16[1,8,16,128]{3,2,1,0:T(8,128)(2,1)S(1)} %collective-permute-done.6.rows_ref), custom_call_target="tpu_custom_call" | custom-call | flops 16777216 | bytes 262144 | tf_op jit(solution)/shard_map/pallas_call | solution.py:134
  17.8 0.3 %collective-permute-start.7 = (f32[2,8,8,128]{3,2,1,0:T(8,128)S(1)}, f32[2,8,8,128]{3,2,1,0:T(8,128)S(1)}, u32[]{:S(2)}, u32[]{:S(2)}) collective-permute-start(f32[2,8,8,128]{3,2,1,0:T(8,128)S(1)} %shard_map.30), channel_id=1, source_target_pairs={{0,2},{2,0},{4,6},{6,4},{8,10},{10,8},{12,14},{14,12},{16,18},{18,... | collective-permute-start | bytes 196616 | tf_op jit(solution)/shard_map/ppermute | solution.py:163
  18.1 0.2 %shard_map.29 = f32[2,8,8,128]{3,2,1,0:T(8,128)S(1)} custom-call(bf16[8,8,16,128]{3,2,1,0:T(8,128)(2,1)S(1)} %constant_dynamic-update-slice_fusion.held_ref, bf16[1,8,16,128]{3,2,1,0:T(8,128)(2,1)S(1)} %get-tuple-element.14.rows_ref), custom_call_target="tpu_custom_call" | custom-call | flops 16777216 | bytes 262144 | tf_op jit(solution)/shard_map/pallas_call | solution.py:134
  18.3 0.8 %collective-permute-done.7 = f32[2,8,8,128]{3,2,1,0:T(8,128)S(1)} collective-permute-done((f32[2,8,8,128]{3,2,1,0:T(8,128)S(1)}, f32[2,8,8,128]{3,2,1,0:T(8,128)S(1)}, u32[]{:S(2)}, u32[]{:S(2)}) %collective-permute-start.7) | collective-permute-done | bytes 65568 | tf_op jit(solution)/shard_map/ppermute | solution.py:163
  19.1 0.6 %add.11 = f32[2,8,8,128]{3,2,1,0:T(8,128)} add(f32[2,8,8,128]{3,2,1,0:T(8,128)S(1)} %shard_map.29, f32[2,8,8,128]{3,2,1,0:T(8,128)S(1)} %collective-permute-done.7) | non-fusion elementwise | flops 16384 | bytes 196608 | tf_op jit(solution)/shard_map/add | solution.py:184
  (6 shorter events, 0.1 us)
Async XLA Ops:
  1.3 5.2 %collective-permute-start = (bf16[8,16,128]{2,1,0:T(8,128)(2,1)S(1)}, bf16[8,16,128]{2,1,0:T(8,128)(2,1)S(1)}, u32[]{:S(2)}, u32[]{:S(2)}) collective-permute-start(bf16[8,16,128]{2,1,0:T(8,128)(2,1)S(1)} %bitcast.11), channel_id=1, source_target_pairs={{0,1},{1,0},{2,3},{3,2},{4,5},{5,4},{6,7},{7,6},{8,9},{9,8},{10,11... | collective-permute-start | bytes 98312 | tf_op jit(solution)/shard_map/ppermute | solution.py:176
  4.4 5.2 %collective-permute-start.2 = (bf16[8,16,128]{2,1,0:T(8,128)(2,1)S(1)}, bf16[8,16,128]{2,1,0:T(8,128)(2,1)S(1)}, u32[]{:S(2)}, u32[]{:S(2)}) collective-permute-start(bf16[8,16,128]{2,1,0:T(8,128)(2,1)S(1)} %bitcast.12), channel_id=1, source_target_pairs={{0,19},{1,18},{2,17},{3,16},{4,23},{5,22},{6,21},{7,20},{8,27},{9,... | collective-permute-start | bytes 98312 | tf_op jit(solution)/shard_map/ppermute | solution.py:177
  6.1 4.2 %collective-permute-start.1 = (bf16[8,16,128]{2,1,0:T(8,128)(2,1)S(1)}, bf16[8,16,128]{2,1,0:T(8,128)(2,1)S(1)}, u32[]{:S(2)}, u32[]{:S(2)}) collective-permute-start(bf16[8,16,128]{2,1,0:T(8,128)(2,1)S(1)} %get-tuple-element.10), channel_id=1, source_target_pairs={{0,18},{2,16},{4,22},{6,20},{8,26},{10,24},{12,30},{14,28},{16,2},... | collective-permute-start | bytes 98312 | tf_op jit(solution)/shard_map/ppermute | solution.py:163
  10.3 4.3 %collective-permute-start.3 = (bf16[2,8,16,128]{3,2,1,0:T(8,128)(2,1)S(1)}, bf16[2,8,16,128]{3,2,1,0:T(8,128)(2,1)S(1)}, u32[]{:S(2)}, u32[]{:S(2)}) collective-permute-start(bf16[2,8,16,128]{3,2,1,0:T(8,128)(2,1)S(1)} %pad_maximum_fusion), channel_id=1, source_target_pairs={{0,4},{2,14},{4,0},{6,10},{8,12},{10,6},{12,8},{14,2},{16,20},{18,... | collective-permute-start | bytes 196616 | tf_op jit(solution)/shard_map/ppermute | solution.py:163
  11.9 5.3 %collective-permute-start.4 = (bf16[2,8,16,128]{3,2,1,0:T(8,128)(2,1)S(1)}, bf16[2,8,16,128]{3,2,1,0:T(8,128)(2,1)S(1)}, u32[]{:S(2)}, u32[]{:S(2)}) collective-permute-start(bf16[2,8,16,128]{3,2,1,0:T(8,128)(2,1)S(1)} %pad_maximum_fusion), channel_id=1, source_target_pairs={{0,12},{2,6},{4,8},{6,2},{8,4},{10,14},{12,0},{14,10},{16,28},{18,... | collective-permute-start | bytes 196616 | tf_op jit(solution)/shard_map/ppermute | solution.py:163
  13.5 4.0 %collective-permute-start.5 = (bf16[2,8,16,128]{3,2,1,0:T(8,128)(2,1)S(1)}, bf16[2,8,16,128]{3,2,1,0:T(8,128)(2,1)S(1)}, u32[]{:S(2)}, u32[]{:S(2)}) collective-permute-start(bf16[2,8,16,128]{3,2,1,0:T(8,128)(2,1)S(1)} %pad_maximum_fusion), channel_id=1, source_target_pairs={{0,10},{2,8},{4,14},{6,12},{8,2},{10,0},{12,6},{14,4},{16,26},{18,... | collective-permute-start | bytes 196616 | tf_op jit(solution)/shard_map/ppermute | solution.py:163
  14.1 3.4 %collective-permute-start.6 = (bf16[1,8,16,128]{3,2,1,0:T(8,128)(2,1)S(1)}, bf16[1,8,16,128]{3,2,1,0:T(8,128)(2,1)S(1)}, u32[]{:S(2)}, u32[]{:S(2)}) collective-permute-start(bf16[1,8,16,128]{3,2,1,0:T(8,128)(2,1)S(1)} %get-tuple-element.14.rows_ref), channel_id=1, source_target_pairs={{0,2},{2,0},{4,6},{6,4},{8,10},{10,8},{12,14},{14,12},{16,18},{18,... | collective-permute-start | bytes 98312 | tf_op jit(solution)/shard_map/ppermute | solution.py:163
  17.8 1.3 %collective-permute-start.7 = (f32[2,8,8,128]{3,2,1,0:T(8,128)S(1)}, f32[2,8,8,128]{3,2,1,0:T(8,128)S(1)}, u32[]{:S(2)}, u32[]{:S(2)}) collective-permute-start(f32[2,8,8,128]{3,2,1,0:T(8,128)S(1)} %shard_map.30), channel_id=1, source_target_pairs={{0,2},{2,0},{4,6},{6,4},{8,10},{10,8},{12,14},{14,12},{16,18},{18,... | collective-permute-start | bytes 196616 | tf_op jit(solution)/shard_map/ppermute | solution.py:163

commit v8 on v7

--- a/solution.py
+++ b/solution.py
@@ -77,16 +77,16 @@
     index, flip, size = 0, 0, 1
     for routes in stages:
         bits = sorted({x for route in routes for x in route[:2] if x & (x - 1) == 0})
-        spots, flips = [0, 0], [0, 0]
+        low, mask = bits[0].bit_length() - 1, 2 ** len(bits) - 1
+        codes = [0, 0]
         for at, route in enumerate(routes):
             for mine in range(2):
-                key = sum(1 << j for j, b in enumerate(bits) if route[mine ^ route[2]] & b)
-                spots[mine] |= (at + 1) << (2 * key)
-                flips[mine] |= route[2] << key
-        key = sum(((chip >> (b.bit_length() - 1)) & 1) << j for j, b in enumerate(bits))
-        spot = jnp.where(core == 0, spots[0], spots[1]) if spots[0] != spots[1] else spots[0]
-        index = index + ((spot >> (2 * key)) & 3) * size
-        flip = flip ^ ((flips[0] >> key) & 1)
+                key = (route[mine ^ route[2]] >> low) & mask
+                codes[mine] |= (4 * route[2] + at + 1) << (4 * key)
+        code = jnp.where(core == 0, codes[0], codes[1]) if codes[0] != codes[1] else codes[0]
+        code = (code >> (4 * ((chip >> low) & mask))) & 7
+        index = index + (code & 3) * size
+        flip = flip ^ (code >> 2)
         size *= len(routes) + 1
     return index, flip
 

time: 19.8 us -> 19.8 us (level)
  no operation moved by 1% of the time
where the time goes in v8:
time: 19.8 us; the launch traced here: 19.7 us
  starting transfers between devices  9.27 us (47%)
  waiting for transfers between devices  7.85 us (40%)
  Pallas kernels  1.8 us (9%)
  other arithmetic  0.68 us (3%)
    ppermute x6, waiting for transfers between devices, across(): return lax.ppermute(block, 'stn', pairs)  4.81 us
    ppermute x6, starting transfers between devices, across(): return lax.ppermute(block, 'stn', pairs)  4.54 us
    ppermute x1, waiting for transfers between devices, body(): lax.ppermute(sent[step - 1], ('stn', 'elem'), there).astype(jnp.float32)  3.05 us
    ppermute x1, starting transfers between devices, body(): mine = mine + lax.ppermute(sent[step - 1], 'elem', here).astype(jnp.float32)  3.03 us
    ppermute x1, starting transfers between devices, body(): lax.ppermute(sent[step - 1], ('stn', 'elem'), there).astype(jnp.float32)  1.69 us
    pallas_call x1, Pallas kernels, partial_beams(): pl.pallas_call(functools.partial(beam_kernel, parts), in_specs=[pl.BlockS...  1.33 us
    add x1, other arithmetic, body(): half_spectra(held, own, [[first]] + stages)  0.64 us
    pallas_call x2, Pallas kernels, half_spectra(): pl.pallas_call(functools.partial(spectra_kernel, stages), out_shape=jax.S...  0.48 us
  transfers between devices with their start and end apart: 8, of which 6 were waited for; matrix products, arithmetic and copies ran while one was open for 0% of the time, Pallas kernels for 1%

profile of v8, /device:TPU:0, one launch (start us, length us, event | category | flops | bytes accessed | tf_op | source)
XLA Modules:
  0.0 19.7 jit_solution(9150775072470290634)
XLA Ops:
  0.0 1.3 %shard_map.28 = (f32[8,16,128]{2,1,0:T(8,128)S(1)}, bf16[8,16,128]{2,1,0:T(8,128)(2,1)S(1)}, bf16[1,8,16,128]{3,2,1,0:T(8,128)(2,1)S(1)}) custom-call(bf16[2,32,16,128]{3,2,1,0:T(8,128)(2,1)} %bitcast.13, bf16[256,32]{1,0:T(8,128)(2,1)} %bitcast.14), custom_call_target="tpu_custom_call" | custom-call | tf_op jit(solution)/shard_map/pallas_call | solution.py:56
  1.3 3.0 %collective-permute-start = (bf16[8,16,128]{2,1,0:T(8,128)(2,1)S(1)}, bf16[8,16,128]{2,1,0:T(8,128)(2,1)S(1)}, u32[]{:S(2)}, u32[]{:S(2)}) collective-permute-start(bf16[8,16,128]{2,1,0:T(8,128)(2,1)S(1)} %bitcast.11), channel_id=1, source_target_pairs={{0,1},{1,0},{2,3},{3,2},{4,5},{5,4},{6,7},{7,6},{8,9},{9,8},{10,11... | collective-permute-start | bytes 98312 | tf_op jit(solution)/shard_map/ppermute | solution.py:176
  4.4 1.7 %collective-permute-start.2 = (bf16[8,16,128]{2,1,0:T(8,128)(2,1)S(1)}, bf16[8,16,128]{2,1,0:T(8,128)(2,1)S(1)}, u32[]{:S(2)}, u32[]{:S(2)}) collective-permute-start(bf16[8,16,128]{2,1,0:T(8,128)(2,1)S(1)} %bitcast.12), channel_id=1, source_target_pairs={{0,19},{1,18},{2,17},{3,16},{4,23},{5,22},{6,21},{7,20},{8,27},{9,... | collective-permute-start | bytes 98312 | tf_op jit(solution)/shard_map/ppermute | solution.py:177
  6.1 0.5 %collective-permute-start.1 = (bf16[8,16,128]{2,1,0:T(8,128)(2,1)S(1)}, bf16[8,16,128]{2,1,0:T(8,128)(2,1)S(1)}, u32[]{:S(2)}, u32[]{:S(2)}) collective-permute-start(bf16[8,16,128]{2,1,0:T(8,128)(2,1)S(1)} %get-tuple-element.10), channel_id=1, source_target_pairs={{0,18},{2,16},{4,22},{6,20},{8,26},{10,24},{12,30},{14,28},{16,2},... | collective-permute-start | bytes 98312 | tf_op jit(solution)/shard_map/ppermute | solution.py:163
  6.5 0.0 collective-permute-done
  6.6 3.0 %collective-permute-done.2 = bf16[8,16,128]{2,1,0:T(8,128)(2,1)S(1)} collective-permute-done((bf16[8,16,128]{2,1,0:T(8,128)(2,1)S(1)}, bf16[8,16,128]{2,1,0:T(8,128)(2,1)S(1)}, u32[]{:S(2)}, u32[]{:S(2)}) %collective-permute-start.2) | collective-permute-done | bytes 32800 | tf_op jit(solution)/shard_map/ppermute | solution.py:177
  9.6 0.7 %collective-permute-done.1 = bf16[8,16,128]{2,1,0:T(8,128)(2,1)S(1)} collective-permute-done((bf16[8,16,128]{2,1,0:T(8,128)(2,1)S(1)}, bf16[8,16,128]{2,1,0:T(8,128)(2,1)S(1)}, u32[]{:S(2)}, u32[]{:S(2)}) %collective-permute-start.1) | collective-permute-done | bytes 32800 | tf_op jit(solution)/shard_map/ppermute | solution.py:163
  10.3 1.6 %collective-permute-start.3 = (bf16[2,8,16,128]{3,2,1,0:T(8,128)(2,1)S(1)}, bf16[2,8,16,128]{3,2,1,0:T(8,128)(2,1)S(1)}, u32[]{:S(2)}, u32[]{:S(2)}) collective-permute-start(bf16[2,8,16,128]{3,2,1,0:T(8,128)(2,1)S(1)} %pad_maximum_fusion), channel_id=1, source_target_pairs={{0,4},{2,14},{4,0},{6,10},{8,12},{10,6},{12,8},{14,2},{16,20},{18,... | collective-permute-start | bytes 196616 | tf_op jit(solution)/shard_map/ppermute | solution.py:163
  11.9 1.6 %collective-permute-start.4 = (bf16[2,8,16,128]{3,2,1,0:T(8,128)(2,1)S(1)}, bf16[2,8,16,128]{3,2,1,0:T(8,128)(2,1)S(1)}, u32[]{:S(2)}, u32[]{:S(2)}) collective-permute-start(bf16[2,8,16,128]{3,2,1,0:T(8,128)(2,1)S(1)} %pad_maximum_fusion), channel_id=1, source_target_pairs={{0,12},{2,6},{4,8},{6,2},{8,4},{10,14},{12,0},{14,10},{16,28},{18,... | collective-permute-start | bytes 196616 | tf_op jit(solution)/shard_map/ppermute | solution.py:163
  13.5 0.7 %collective-permute-start.5 = (bf16[2,8,16,128]{3,2,1,0:T(8,128)(2,1)S(1)}, bf16[2,8,16,128]{3,2,1,0:T(8,128)(2,1)S(1)}, u32[]{:S(2)}, u32[]{:S(2)}) collective-permute-start(bf16[2,8,16,128]{3,2,1,0:T(8,128)(2,1)S(1)} %pad_maximum_fusion), channel_id=1, source_target_pairs={{0,10},{2,8},{4,14},{6,12},{8,2},{10,0},{12,6},{14,4},{16,26},{18,... | collective-permute-start | bytes 196616 | tf_op jit(solution)/shard_map/ppermute | solution.py:163
  14.1 0.0 collective-permute-start.6
  14.1 0.5 %collective-permute-done.3 = bf16[2,8,16,128]{3,2,1,0:T(8,128)(2,1)S(1)} collective-permute-done((bf16[2,8,16,128]{3,2,1,0:T(8,128)(2,1)S(1)}, bf16[2,8,16,128]{3,2,1,0:T(8,128)(2,1)S(1)}, u32[]{:S(2)}, u32[]{:S(2)}) %collective-permute-start.3) | collective-permute-done | bytes 65568 | tf_op jit(solution)/shard_map/ppermute | solution.py:163
  14.7 2.5 %collective-permute-done.4 = bf16[2,8,16,128]{3,2,1,0:T(8,128)(2,1)S(1)} collective-permute-done((bf16[2,8,16,128]{3,2,1,0:T(8,128)(2,1)S(1)}, bf16[2,8,16,128]{3,2,1,0:T(8,128)(2,1)S(1)}, u32[]{:S(2)}, u32[]{:S(2)}) %collective-permute-start.4) | collective-permute-done | bytes 65568 | tf_op jit(solution)/shard_map/ppermute | solution.py:163
  17.2 0.3 %collective-permute-done.5 = bf16[2,8,16,128]{3,2,1,0:T(8,128)(2,1)S(1)} collective-permute-done((bf16[2,8,16,128]{3,2,1,0:T(8,128)(2,1)S(1)}, bf16[2,8,16,128]{3,2,1,0:T(8,128)(2,1)S(1)}, u32[]{:S(2)}, u32[]{:S(2)}) %collective-permute-start.5) | collective-permute-done | bytes 65568 | tf_op jit(solution)/shard_map/ppermute | solution.py:163
  17.5 0.0 collective-permute-done.6.rows_ref
  17.5 0.2 %shard_map.30 = f32[2,8,8,128]{3,2,1,0:T(8,128)S(1)} custom-call(bf16[8,8,16,128]{3,2,1,0:T(8,128)(2,1)S(1)} %constant_dynamic-update-slice_fusion.held_ref, bf16[1,8,16,128]{3,2,1,0:T(8,128)(2,1)S(1)} %collective-permute-done.6.rows_ref), custom_call_target="tpu_custom_call" | custom-call | flops 16777216 | bytes 262144 | tf_op jit(solution)/shard_map/pallas_call | solution.py:134
  17.8 0.3 %collective-permute-start.7 = (f32[2,8,8,128]{3,2,1,0:T(8,128)S(1)}, f32[2,8,8,128]{3,2,1,0:T(8,128)S(1)}, u32[]{:S(2)}, u32[]{:S(2)}) collective-permute-start(f32[2,8,8,128]{3,2,1,0:T(8,128)S(1)} %shard_map.30), channel_id=1, source_target_pairs={{0,2},{2,0},{4,6},{6,4},{8,10},{10,8},{12,14},{14,12},{16,18},{18,... | collective-permute-start | bytes 196616 | tf_op jit(solution)/shard_map/ppermute | solution.py:163
  18.0 0.2 %shard_map.29 = f32[2,8,8,128]{3,2,1,0:T(8,128)S(1)} custom-call(bf16[8,8,16,128]{3,2,1,0:T(8,128)(2,1)S(1)} %constant_dynamic-update-slice_fusion.held_ref, bf16[1,8,16,128]{3,2,1,0:T(8,128)(2,1)S(1)} %get-tuple-element.14.rows_ref), custom_call_target="tpu_custom_call" | custom-call | flops 16777216 | bytes 262144 | tf_op jit(solution)/shard_map/pallas_call | solution.py:134
  18.3 0.8 %collective-permute-done.7 = f32[2,8,8,128]{3,2,1,0:T(8,128)S(1)} collective-permute-done((f32[2,8,8,128]{3,2,1,0:T(8,128)S(1)}, f32[2,8,8,128]{3,2,1,0:T(8,128)S(1)}, u32[]{:S(2)}, u32[]{:S(2)}) %collective-permute-start.7) | collective-permute-done | bytes 65568 | tf_op jit(solution)/shard_map/ppermute | solution.py:163
  19.0 0.6 %add.11 = f32[2,8,8,128]{3,2,1,0:T(8,128)} add(f32[2,8,8,128]{3,2,1,0:T(8,128)S(1)} %shard_map.29, f32[2,8,8,128]{3,2,1,0:T(8,128)S(1)} %collective-permute-done.7) | non-fusion elementwise | flops 16384 | bytes 196608 | tf_op jit(solution)/shard_map/add | solution.py:184
  (6 shorter events, 0.1 us)
Async XLA Ops:
  1.3 5.2 %collective-permute-start = (bf16[8,16,128]{2,1,0:T(8,128)(2,1)S(1)}, bf16[8,16,128]{2,1,0:T(8,128)(2,1)S(1)}, u32[]{:S(2)}, u32[]{:S(2)}) collective-permute-start(bf16[8,16,128]{2,1,0:T(8,128)(2,1)S(1)} %bitcast.11), channel_id=1, source_target_pairs={{0,1},{1,0},{2,3},{3,2},{4,5},{5,4},{6,7},{7,6},{8,9},{9,8},{10,11... | collective-permute-start | bytes 98312 | tf_op jit(solution)/shard_map/ppermute | solution.py:176
  4.4 5.2 %collective-permute-start.2 = (bf16[8,16,128]{2,1,0:T(8,128)(2,1)S(1)}, bf16[8,16,128]{2,1,0:T(8,128)(2,1)S(1)}, u32[]{:S(2)}, u32[]{:S(2)}) collective-permute-start(bf16[8,16,128]{2,1,0:T(8,128)(2,1)S(1)} %bitcast.12), channel_id=1, source_target_pairs={{0,19},{1,18},{2,17},{3,16},{4,23},{5,22},{6,21},{7,20},{8,27},{9,... | collective-permute-start | bytes 98312 | tf_op jit(solution)/shard_map/ppermute | solution.py:177
  6.1 4.2 %collective-permute-start.1 = (bf16[8,16,128]{2,1,0:T(8,128)(2,1)S(1)}, bf16[8,16,128]{2,1,0:T(8,128)(2,1)S(1)}, u32[]{:S(2)}, u32[]{:S(2)}) collective-permute-start(bf16[8,16,128]{2,1,0:T(8,128)(2,1)S(1)} %get-tuple-element.10), channel_id=1, source_target_pairs={{0,18},{2,16},{4,22},{6,20},{8,26},{10,24},{12,30},{14,28},{16,2},... | collective-permute-start | bytes 98312 | tf_op jit(solution)/shard_map/ppermute | solution.py:163
  10.3 4.3 %collective-permute-start.3 = (bf16[2,8,16,128]{3,2,1,0:T(8,128)(2,1)S(1)}, bf16[2,8,16,128]{3,2,1,0:T(8,128)(2,1)S(1)}, u32[]{:S(2)}, u32[]{:S(2)}) collective-permute-start(bf16[2,8,16,128]{3,2,1,0:T(8,128)(2,1)S(1)} %pad_maximum_fusion), channel_id=1, source_target_pairs={{0,4},{2,14},{4,0},{6,10},{8,12},{10,6},{12,8},{14,2},{16,20},{18,... | collective-permute-start | bytes 196616 | tf_op jit(solution)/shard_map/ppermute | solution.py:163
  11.9 5.3 %collective-permute-start.4 = (bf16[2,8,16,128]{3,2,1,0:T(8,128)(2,1)S(1)}, bf16[2,8,16,128]{3,2,1,0:T(8,128)(2,1)S(1)}, u32[]{:S(2)}, u32[]{:S(2)}) collective-permute-start(bf16[2,8,16,128]{3,2,1,0:T(8,128)(2,1)S(1)} %pad_maximum_fusion), channel_id=1, source_target_pairs={{0,12},{2,6},{4,8},{6,2},{8,4},{10,14},{12,0},{14,10},{16,28},{18,... | collective-permute-start | bytes 196616 | tf_op jit(solution)/shard_map/ppermute | solution.py:163
  13.5 4.0 %collective-permute-start.5 = (bf16[2,8,16,128]{3,2,1,0:T(8,128)(2,1)S(1)}, bf16[2,8,16,128]{3,2,1,0:T(8,128)(2,1)S(1)}, u32[]{:S(2)}, u32[]{:S(2)}) collective-permute-start(bf16[2,8,16,128]{3,2,1,0:T(8,128)(2,1)S(1)} %pad_maximum_fusion), channel_id=1, source_target_pairs={{0,10},{2,8},{4,14},{6,12},{8,2},{10,0},{12,6},{14,4},{16,26},{18,... | collective-permute-start | bytes 196616 | tf_op jit(solution)/shard_map/ppermute | solution.py:163
  14.1 3.4 %collective-permute-start.6 = (bf16[1,8,16,128]{3,2,1,0:T(8,128)(2,1)S(1)}, bf16[1,8,16,128]{3,2,1,0:T(8,128)(2,1)S(1)}, u32[]{:S(2)}, u32[]{:S(2)}) collective-permute-start(bf16[1,8,16,128]{3,2,1,0:T(8,128)(2,1)S(1)} %get-tuple-element.14.rows_ref), channel_id=1, source_target_pairs={{0,2},{2,0},{4,6},{6,4},{8,10},{10,8},{12,14},{14,12},{16,18},{18,... | collective-permute-start | bytes 98312 | tf_op jit(solution)/shard_map/ppermute | solution.py:163
  17.8 1.3 %collective-permute-start.7 = (f32[2,8,8,128]{3,2,1,0:T(8,128)S(1)}, f32[2,8,8,128]{3,2,1,0:T(8,128)S(1)}, u32[]{:S(2)}, u32[]{:S(2)}) collective-permute-start(f32[2,8,8,128]{3,2,1,0:T(8,128)S(1)} %shard_map.30), channel_id=1, source_target_pairs={{0,2},{2,0},{4,6},{6,4},{8,10},{10,8},{12,14},{14,12},{16,18},{18,... | collective-permute-start | bytes 196616 | tf_op jit(solution)/shard_map/ppermute | solution.py:163
